TPU v7x, 256 devices: a whole 4x4x8 slice. The times are simulated.
256 devices in a mesh: dec: 32 (over y, x, core), ch: 8 (over z).
Axes of the slice: x: 4, y: 4, z: 8, core: 2. Of those that a mesh axis runs over, the one named last changes fastest.
Arguments:
- frame_cotangent: bfloat16 [256, 160, 8192], P('dec', None, 'ch'), may hold values from -5 to 5
- rollout_utterance: int32 [256], P('dec'), may hold values from 0 to 31, as said below
- frame_offset: int32 [256], P('dec'), may hold values from 0 to 32
- utterance_frames: int32 [32], P('dec'), may hold values from 1 to 128, 3072 in all
- normed_input: bfloat16 [32, 128, 1024], P('dec', None, 'ch'), may hold values from -6 to 6
- expand_weight: bfloat16 [1024, 2, 1024], P(None, None, 'ch'), may hold values from -0.1875 to 0.1875
- depth_kernel: bfloat16 [9, 1024], P(None, 'ch'), may hold values from -2 to 2
- norm_scale: float32 [1024], P('ch'), may hold values from 0.1 to 1.9
- norm_shift: float32 [1024], P('ch'), may hold values from -3 to 3
- project_weight: bfloat16 [1024, 1024], replicated, may hold values from -0.1875 to 0.1875
- adapter_weight: bfloat16 [1024, 8192], P(None, 'ch'), may hold values from -0.0625 to 0.0625
Outputs:
- grad_stream: bfloat16 [32, 128, 1024], P('dec', None, 'ch')
- grad_normed: bfloat16 [32, 128, 1024], P('dec', None, 'ch')
Inputs may be any that keep to these rules, and one draw needn't show every extreme that they name: `rollout_utterance`: each utterance is named by exactly 8 rollouts; utterances k * 1 to (k + 1) - 1 are owned by index k of dec; among the 8 rollouts of one index of dec at most 1 name utterances of one owner, and some owner is named exactly 1 times; the rollouts of index k of dec always name some utterance of the owner (k + 16) mod 32.
All inputs are finite; a program needn't handle non-finite values. No bound on the sum of `utterance_frames` on one device may be relied on, other than what follows from the above.
Results may differ from a plain program's by a relative error of at most 0.03.
Values may be sent and summed in bfloat16 or wider, within the bound.
A program may use at most 128 MiB of HBM per device.

v0:
```python
import jax
import jax.numpy as jnp
from jax import lax
from jax.sharding import PartitionSpec as P


def body(
    frame_cotangent,
    rollout_utterance,
    frame_offset,
    utterance_frames,
    normed_input,
    expand_weight,
    depth_kernel,
    norm_scale,
    norm_shift,
    project_weight,
    adapter_weight,
):
    local_rolls, seq_len, d_local = frame_cotangent.shape
    u_local, frames, c_local = normed_input.shape
    width = expand_weight.shape[0]
    taps = depth_kernel.shape[0]
    row_count = u_local * frames
    slabs = jax.vmap(lambda window, first: lax.dynamic_slice_in_dim(window, first, frames, 0))(
        frame_cotangent, frame_offset
    )
    flat_slabs = slabs.reshape(local_rolls, frames * d_local)
    target = jnp.arange(lax.axis_size("dec") * u_local, dtype=jnp.int32)
    select = (target[:, None] == rollout_utterance[None, :]).astype(jnp.bfloat16)
    rounded = lax.optimization_barrier(
        jnp.dot(select, flat_slabs, preferred_element_type=jnp.float32).astype(jnp.bfloat16)
    )
    received = lax.psum_scatter(
        rounded.astype(jnp.float32).astype(jnp.bfloat16), "dec", scatter_dimension=0, tiled=True
    ).astype(jnp.float32)
    frame_index = jnp.arange(frames, dtype=jnp.int32)
    mask = (frame_index[None, :] < utterance_frames[:, None]).astype(jnp.float32)
    frame_grad = (received.reshape(u_local, frames, d_local) * mask[:, :, None]).astype(
        jnp.bfloat16
    )
    grad_rows = frame_grad.reshape(row_count, d_local)
    block = adapter_weight
    stream_cols = lax.psum_scatter(
        lax.dot_general(
            block, grad_rows, (((1,), (1,)), ((), ())), preferred_element_type=jnp.float32
        ).astype(jnp.bfloat16),
        "ch",
        scatter_dimension=0,
        tiled=True,
    ).astype(jnp.float32)
    grad_stream = stream_cols.T.astype(jnp.bfloat16)
    expand_flat = expand_weight.reshape(width, 2 * c_local)
    piece = lax.all_gather(normed_input, "ch", axis=2, tiled=True)
    span = piece.shape[2]
    block = expand_flat
    expanded = jnp.dot(piece.reshape(row_count, span), block, preferred_element_type=jnp.float32)
    value = expanded[:, :c_local]
    gate = expanded[:, c_local:]
    sig_gate = jax.nn.sigmoid(gate)
    mask_rows = mask.reshape(row_count, 1)
    glu = (mask_rows * value * sig_gate).reshape(u_local, frames, c_local)
    kernel = depth_kernel.astype(jnp.float32)
    half = (taps - 1) // 2
    padded = jnp.pad(glu, ((0, 0), (half, half), (0, 0)))
    depth = jnp.zeros((u_local, frames, c_local), jnp.float32)
    for step in range(taps):
        depth = depth + kernel[step] * padded[:, step : step + frames, :]
    shifted = depth * norm_scale + norm_shift
    ch_start = lax.axis_index("ch") * c_local
    own_rows = lax.dynamic_slice_in_dim(project_weight, ch_start, c_local, 0)
    grad_swish = lax.dot_general(
        lax.all_gather(grad_stream, "ch", axis=1, tiled=True),
        own_rows,
        (((1,), (1,)), ((), ())),
        preferred_element_type=jnp.float32,
    )
    grad_swish = grad_swish.reshape(u_local, frames, c_local)
    sig_shift = jax.nn.sigmoid(shifted)
    grad_depth = grad_swish * sig_shift * (1.0 + shifted * (1.0 - sig_shift)) * norm_scale
    padded_back = jnp.pad(grad_depth, ((0, 0), (half, half), (0, 0)))
    grad_glu = jnp.zeros((u_local, frames, c_local), jnp.float32)
    for step in range(taps):
        grad_glu = (
            grad_glu + kernel[step] * padded_back[:, taps - 1 - step : taps - 1 - step + frames, :]
        )
    grad_glu = grad_glu.reshape(row_count, c_local) * mask_rows
    grad_value = grad_glu * sig_gate
    grad_gate = grad_glu * value * sig_gate * (1.0 - sig_gate)
    grad_expanded = jnp.concatenate([grad_value, grad_gate], axis=1).astype(jnp.bfloat16)
    block = expand_flat
    input_cols = lax.psum_scatter(
        lax.dot_general(
            block, grad_expanded, (((1,), (1,)), ((), ())), preferred_element_type=jnp.float32
        ).astype(jnp.bfloat16),
        "ch",
        scatter_dimension=0,
        tiled=True,
    ).astype(jnp.float32)
    grad_normed = input_cols.T.astype(jnp.bfloat16)
    return (
        grad_stream.reshape(u_local, frames, c_local),
        grad_normed.reshape(u_local, frames, c_local),
    )


def solution(mesh):
    return jax.shard_map(
        body,
        mesh=mesh,
        in_specs=(
            P("dec", None, "ch"),
            P("dec"),
            P("dec"),
            P("dec"),
            P("dec", None, "ch"),
            P(None, None, "ch"),
            P(None, "ch"),
            P("ch"),
            P("ch"),
            P(),
            P(None, "ch"),
        ),
        out_specs=(P("dec", None, "ch"), P("dec", None, "ch")),
        check_vma=False,
    )
```

profile of v0, /device:TPU:1, one launch (start us, length us, event | category | flops | bytes accessed | tf_op | source)
XLA Modules:
  0.0 286.5 jit_solution(7985115832883132730)
XLA Ops:
  7.2 0.0 copy-start
  7.2 0.0 all-reduce.6.cloned.1.call-start
  7.2 0.8 fusion.34
  8.0 29.7 %while.1 = (s32[]{:T(128)}, bf16[8,160,1024]{2,1,0:T(8,128)(2,1)}, s32[8,3]{0,1:T(4,128)S(1)}, bf16[8,128,1024]{2,1,0:T(8,128)(2,1)}, s32[]{:T(128)}) while((s32[]{:T(128)}, bf16[8,160,1024]{2,1,0:T(8,128)(2,1)}, s32[8,3]{0,1:T(4,128)S(1)}, bf16[8,128,1024]{2,1,0:T(8,128)(2,1)}, s32[]{:T(128)}) %tuple.32), condition=%wide.while_cond, body=%wide.while_body.sunk | while | flops 2 | bytes 525429 | solution.py:25
  8.1 0.1 constant_dynamic-slice_fusion.2
  8.1 0.6 fusion.42
  8.7 3.1 %dynamic-slice_dynamic-update-slice_fusion.2 = bf16[8,128,1024]{2,1,0:T(8,128)(2,1)} fusion(bf16[8,128,1024]{2,1,0:T(8,128)(2,1)} %get-tuple-element.68, s32[]{:T(128)S(6)} %copy.30, bf16[8,160,1024]{2,1,0:T(8,128)(2,1)} %get-tuple-element.71, s32[]{:T(128)} %bitcast.81, s32[]{:T(128)} %bitcast.82), kind=kLoop, calls=%fused_computation.clone.1 | loop fusion | bytes 525316 | tf_op jit(solution)/shard_map/vmap()/gather
  11.8 0.1 constant_dynamic-slice_fusion.2
  11.8 0.6 fusion.42
  12.4 3.0 %dynamic-slice_dynamic-update-slice_fusion.2 = bf16[8,128,1024]{2,1,0:T(8,128)(2,1)} fusion(bf16[8,128,1024]{2,1,0:T(8,128)(2,1)} %get-tuple-element.68, s32[]{:T(128)S(6)} %copy.30, bf16[8,160,1024]{2,1,0:T(8,128)(2,1)} %get-tuple-element.71, s32[]{:T(128)} %bitcast.81, s32[]{:T(128)} %bitcast.82), kind=kLoop, calls=%fused_computation.clone.1 | loop fusion | bytes 525316 | tf_op jit(solution)/shard_map/vmap()/gather
  15.5 0.1 constant_dynamic-slice_fusion.2
  15.5 0.6 fusion.42
  16.1 3.0 %dynamic-slice_dynamic-update-slice_fusion.2 = bf16[8,128,1024]{2,1,0:T(8,128)(2,1)} fusion(bf16[8,128,1024]{2,1,0:T(8,128)(2,1)} %get-tuple-element.68, s32[]{:T(128)S(6)} %copy.30, bf16[8,160,1024]{2,1,0:T(8,128)(2,1)} %get-tuple-element.71, s32[]{:T(128)} %bitcast.81, s32[]{:T(128)} %bitcast.82), kind=kLoop, calls=%fused_computation.clone.1 | loop fusion | bytes 525316 | tf_op jit(solution)/shard_map/vmap()/gather
  19.2 0.1 constant_dynamic-slice_fusion.2
  19.2 0.6 fusion.42
  19.8 3.0 %dynamic-slice_dynamic-update-slice_fusion.2 = bf16[8,128,1024]{2,1,0:T(8,128)(2,1)} fusion(bf16[8,128,1024]{2,1,0:T(8,128)(2,1)} %get-tuple-element.68, s32[]{:T(128)S(6)} %copy.30, bf16[8,160,1024]{2,1,0:T(8,128)(2,1)} %get-tuple-element.71, s32[]{:T(128)} %bitcast.81, s32[]{:T(128)} %bitcast.82), kind=kLoop, calls=%fused_computation.clone.1 | loop fusion | bytes 525316 | tf_op jit(solution)/shard_map/vmap()/gather
  22.9 0.1 constant_dynamic-slice_fusion.2
  22.9 0.6 fusion.42
  23.5 3.1 %dynamic-slice_dynamic-update-slice_fusion.2 = bf16[8,128,1024]{2,1,0:T(8,128)(2,1)} fusion(bf16[8,128,1024]{2,1,0:T(8,128)(2,1)} %get-tuple-element.68, s32[]{:T(128)S(6)} %copy.30, bf16[8,160,1024]{2,1,0:T(8,128)(2,1)} %get-tuple-element.71, s32[]{:T(128)} %bitcast.81, s32[]{:T(128)} %bitcast.82), kind=kLoop, calls=%fused_computation.clone.1 | loop fusion | bytes 525316 | tf_op jit(solution)/shard_map/vmap()/gather
  26.6 0.1 constant_dynamic-slice_fusion.2
  26.7 0.6 fusion.42
  27.2 3.1 %dynamic-slice_dynamic-update-slice_fusion.2 = bf16[8,128,1024]{2,1,0:T(8,128)(2,1)} fusion(bf16[8,128,1024]{2,1,0:T(8,128)(2,1)} %get-tuple-element.68, s32[]{:T(128)S(6)} %copy.30, bf16[8,160,1024]{2,1,0:T(8,128)(2,1)} %get-tuple-element.71, s32[]{:T(128)} %bitcast.81, s32[]{:T(128)} %bitcast.82), kind=kLoop, calls=%fused_computation.clone.1 | loop fusion | bytes 525316 | tf_op jit(solution)/shard_map/vmap()/gather
  30.3 0.1 constant_dynamic-slice_fusion.2
  30.4 0.6 fusion.42
  31.0 3.1 %dynamic-slice_dynamic-update-slice_fusion.2 = bf16[8,128,1024]{2,1,0:T(8,128)(2,1)} fusion(bf16[8,128,1024]{2,1,0:T(8,128)(2,1)} %get-tuple-element.68, s32[]{:T(128)S(6)} %copy.30, bf16[8,160,1024]{2,1,0:T(8,128)(2,1)} %get-tuple-element.71, s32[]{:T(128)} %bitcast.81, s32[]{:T(128)} %bitcast.82), kind=kLoop, calls=%fused_computation.clone.1 | loop fusion | bytes 525316 | tf_op jit(solution)/shard_map/vmap()/gather
  34.0 0.1 constant_dynamic-slice_fusion.2
  34.1 0.6 fusion.42
  34.7 3.1 %dynamic-slice_dynamic-update-slice_fusion.2 = bf16[8,128,1024]{2,1,0:T(8,128)(2,1)} fusion(bf16[8,128,1024]{2,1,0:T(8,128)(2,1)} %get-tuple-element.68, s32[]{:T(128)S(6)} %copy.30, bf16[8,160,1024]{2,1,0:T(8,128)(2,1)} %get-tuple-element.71, s32[]{:T(128)} %bitcast.81, s32[]{:T(128)} %bitcast.82), kind=kLoop, calls=%fused_computation.clone.1 | loop fusion | bytes 525316 | tf_op jit(solution)/shard_map/vmap()/gather
  37.7 2.8 copy.17
  40.5 0.0 copy-done.5
  40.5 5.5 %convolution_convert_fusion = bf16[32,131072]{1,0:T(8,128)(2,1)} fusion(bf16[8,131072]{1,0:T(8,128)(2,1)S(1)} %bitcast.84, s32[8]{0:T(128)S(1)} %copy-done.5), kind=kOutput, calls=%fused_computation.2 | convolution fusion | flops 71303424 | bytes 10485792 | tf_op jit(solution)/shard_map/dot_general | solution.py:32
  46.1 0.0 all-reduce.6.cloned.1.call-update
  46.1 0.0 reduce-scatter.7.cloned.1.call-start
  46.8 0.0 copy-done.4
  46.8 0.0 copy-done.8
  46.8 0.6 dynamic-slice.4
  47.4 133.3 %all-reduce.6.cloned.1.call-done = bf16[32,131072]{1,0:T(8,128)(2,1)} async-done(((bf16[32,131072]{1,0:T(8,128)(2,1)}), bf16[32,131072]{1,0:T(8,128)(2,1)}) %all-reduce.6.cloned.1.call-update) | async-done | bytes 8388624
  180.7 3.8 %fusion.8 = f32[131072]{0:T(1024)S(1)} fusion(bf16[32,131072]{1,0:T(8,128)(2,1)} %all-reduce.6.cloned.1.call-done, u32[]{:T(128)} %bitcast.26), kind=kLoop, calls=%fused_computation.15 | loop fusion | flops 131072 | bytes 786436 | tf_op jit(solution)/shard_map/reshape | solution.py:39
  184.6 0.1 reshape.134
  184.7 0.0 copy-done
  184.7 0.0 copy-start.3
  184.7 0.0 copy-start.1
  184.7 0.0 copy-start.6
  184.7 0.0 copy-start.7
  184.7 0.8 fusion
  185.6 0.9 copy.13
  186.4 0.0 reduce-scatter.7.cloned.1.call-update
  186.4 0.0 reduce-scatter.9.cloned.1.call-start
  186.5 0.0 copy-done.3
  186.5 20.5 %all_gather.7 = bf16[1,128,1024]{2,1,0:T(8,128)(2,1)S(1)} all-gather(bf16[1,128,128]{2,1,0:T(8,128)(2,1)S(1)} %copy-done.3), channel_id=1, replica_groups=mesh['dec'=32,'ch'=8] {'ch'}, dimensions={2}, use_global_device_ids=true | all-gather | bytes 294912 | tf_op jit(solution)/shard_map/all_gather | solution.py:54
  207.0 0.0 copy-done.1
  207.0 0.2 fusion.6
  207.2 0.1 fusion.33
  207.3 10.5 %reduce-scatter.7.cloned.1.call-done = bf16[128,128]{1,0:T(8,128)(2,1)} async-done(((bf16[1024,128]{1,0:T(8,128)(2,1)}), bf16[128,128]{1,0:T(8,128)(2,1)}) %reduce-scatter.7.cloned.1.call-update) | async-done | bytes 32784
  217.8 0.9 copy.14
  218.6 0.0 copy-start.2
  218.7 17.4 %all_gather.6 = bf16[128,1024]{1,0:T(8,128)(2,1)S(1)} all-gather(bf16[128,128]{1,0:T(8,128)(2,1)S(1)} %bitcast.88), channel_id=1, replica_groups=mesh['dec'=32,'ch'=8] {'ch'}, dimensions={1}, use_global_device_ids=true | all-gather | bytes 294912 | tf_op jit(solution)/shard_map/all_gather | solution.py:73
  236.1 1.2 fusion.4
  237.3 0.1 multiply_convert_fusion.3
  237.4 0.3 fusion.1
  237.7 0.9 copy.15
  238.6 0.0 reduce-scatter.9.cloned.1.call-update
  238.6 39.9 %reduce-scatter.9.cloned.1.call-done = bf16[128,128]{1,0:T(8,128)(2,1)} async-done(((bf16[1024,128]{1,0:T(8,128)(2,1)}), bf16[128,128]{1,0:T(8,128)(2,1)}) %reduce-scatter.9.cloned.1.call-update) | async-done | bytes 32784
  278.5 1.5 copy.16
  (13 shorter events, 0.1 us)
Async XLA Ops:
  7.2 177.5 %copy-start = (bf16[1024,1024]{1,0:T(8,128)(2,1)S(1)}, bf16[1024,1024]{1,0:T(8,128)(2,1)}, u32[]{:S(2)}) copy-start(bf16[1024,1024]{1,0:T(8,128)(2,1)} %param.21) | copy-start | bytes 6291460
  7.2 173.6 %all-reduce.6.cloned.1.call-start = ((), (), s32[]{:S(2)}) async-start(), calls=%async_computation.4 | async-start | bytes 16777216
  37.7 2.8 copy-start.5
  46.0 0.7 copy-start.4
  46.1 0.8 copy-start.8
  46.1 171.7 %reduce-scatter.7.cloned.1.call-start = ((), (), s32[]{:S(2)}) async-start(), calls=%async_computation.2 | async-start | bytes 294912
  184.7 1.8 copy-start.3
  184.7 22.3 %copy-start.1 = (bf16[1024,2,128]{2,1,0:T(2,128)(2,1)S(1)}, bf16[1024,2,128]{2,1,0:T(2,128)(2,1)}, u32[]{:S(2)}) copy-start(bf16[1024,2,128]{2,1,0:T(2,128)(2,1)} %param.16) | copy-start | bytes 1572868
  184.7 51.4 %copy-start.6 = (f32[128]{0:T(128)S(1)}, f32[128]{0:T(128)}, u32[]{:S(2)}) copy-start(f32[128]{0:T(128)} %param.19) | copy-start | bytes 1540
  184.7 51.4 %copy-start.7 = (f32[128]{0:T(128)S(1)}, f32[128]{0:T(128)}, u32[]{:S(2)}) copy-start(f32[128]{0:T(128)} %param.18) | copy-start | bytes 1540
  186.4 92.1 %reduce-scatter.9.cloned.1.call-start = ((), (), s32[]{:S(2)}) async-start(), calls=%async_computation.3 | async-start | bytes 294912
  218.6 61.4 %copy-start.2 = (bf16[128,128]{0,1:T(8,128)(2,1)}, bf16[128,128]{0,1:T(8,128)(2,1)S(1)}, u32[]{:S(2)}) copy-start(bf16[128,128]{0,1:T(8,128)(2,1)S(1)} %copy.14) | copy-start | bytes 98308
Sparse Core Ops, SparseCore 0:
  46.2 134.4 all-reduce.5
  186.5 31.1 reduce-scatter.6
  238.7 39.7 reduce-scatter.8
where the time goes:
time: 292 us; the launch traced here: 287 us
  waiting for transfers between devices  184 us (63%)
  blocking collectives  37.9 us (13%)
  local copies, waits for them, and re-layouts  37.2 us (13%)
  between operations  14.6 us (5%)
  matrix products  8.12 us (3%)
  other arithmetic  4.86 us (2%)
    unnamed x6, waiting for transfers between devices  184 us
    gather x24, local copies, waits for them, and re-layouts  29.7 us
    all_gather x1, blocking collectives, body(): piece = lax.all_gather(normed_input, 'ch', axis=2, tiled=True)  20.5 us
    all_gather x1, blocking collectives, body(): lax.all_gather(grad_stream, 'ch', axis=1, tiled=True)  17.4 us
    unnamed x25, local copies, waits for them, and re-layouts  7.43 us
  transfers between devices with their start and end apart: 3, of which 3 were waited for; matrix products, arithmetic and copies ran while one was open for 0% of the time, Pallas kernels for 0%

commit v1 on v0

v1 whole, which is shorter than its diff:
```python
import jax
import jax.numpy as jnp
from jax import lax
from jax.experimental import pallas as pl
from jax.experimental.pallas import tpu as pltpu
from jax.sharding import PartitionSpec as P

MESH = pl.DeviceIdType.MESH
F32 = jnp.float32
BF16 = jnp.bfloat16
NY, NX, NCORE, NZ = 4, 4, 2, 8
RING = NX * NCORE


def steps(first, last, work):
    def one(step, carry):
        work(step)
        return carry

    lax.fori_loop(first, last, one, 0)


def rows_of(start, size):
    return pl.ds(pl.multiple_of(start, size), size)


def nt(a, b):
    return lax.dot_general(a, b, (((1,), (1,)), ((), ())), preferred_element_type=F32)


def kernel(
    ids_sm,
    offs_sm,
    frames_sm,
    normed_ref,
    taps_ref,
    scale_ref,
    shift_ref,
    cot_hbm,
    expand_hbm,
    project_hbm,
    adapter_hbm,
    stream_out,
    normed_out,
    cot,
    expand2,
    project,
    adapter,
    fused,
    expand,
    slabs,
    landed,
    ids,
    sel_t,
    sel,
    part,
    part_in,
    fg,
    x_all,
    zsend,
    zrecv,
    owned,
    back,
    pad,
    f_gsw,
    f_val,
    f_gate,
    load_sem,
    s1_send,
    s1_recv,
    id_send,
    id_recv,
    s2_send,
    s2_recv,
    z_send,
    z_recv,
    b_send,
    b_recv,
):
    me = lax.axis_index("dec")
    c = lax.axis_index("ch")
    y = lax.div(me, RING)
    pos_a = lax.rem(me, RING)
    x = lax.div(pos_a, NCORE)
    core = lax.rem(pos_a, NCORE)
    pos_b = y * NCORE + core
    positions = (pos_a, pos_b)

    def ring_dev(half, g):
        if half == 0:
            return y * RING + g
        return lax.div(g, NCORE) * RING + x * NCORE + lax.rem(g, NCORE)

    def line_dev(half, q):
        if half == 0:
            return q * RING + pos_a
        return y * RING + q * NCORE + core

    lines = (y, x)

    loads = []
    for r in range(8):
        loads.append(pltpu.make_async_copy(cot_hbm.at[r], cot.at[r], load_sem.at[r]))
    loads.append(pltpu.make_async_copy(project_hbm, project, load_sem.at[8]))
    loads.append(pltpu.make_async_copy(adapter_hbm, adapter, load_sem.at[9]))
    loads.append(pltpu.make_async_copy(expand_hbm, expand2, load_sem.at[10]))
    for load in loads:
        load.start()

    barrier = pltpu.get_barrier_semaphore()

    def greet(device):
        pl.semaphore_signal(barrier, inc=1, device_id=device, device_id_type=MESH)

    steps(1, RING, lambda o: greet((ring_dev(0, lax.rem(pos_a + o, RING)), c)))
    for other in range(NCORE):
        steps(1, NY, lambda o: greet((ring_dev(1, lax.rem(y + o, NY) * NCORE + other), c)))
    steps(1, NZ, lambda o: greet((me, lax.rem(c + o, NZ))))

    row8 = lax.broadcasted_iota(jnp.int32, (8, 128), 0)
    tile = jnp.zeros((8, 128), jnp.int32)
    for r in range(8):
        tile = jnp.where(row8 == r, ids_sm[r], tile)
    ids[0, pos_a] = tile
    ids[1, pos_b] = tile

    srow = lax.broadcasted_iota(jnp.int32, (128, 160), 0)
    scol = lax.broadcasted_iota(jnp.int32, (128, 160), 1)
    diff = scol - srow
    for p in range(4):
        loads[2 * p].wait()
        loads[2 * p + 1].wait()
        sh0 = (diff == offs_sm[2 * p]).astype(F32).astype(BF16)
        sh1 = (diff == offs_sm[2 * p + 1]).astype(F32).astype(BF16)
        for n in range(4):
            cols = slice(n * 256, (n + 1) * 256)
            a = jnp.dot(sh0, cot[2 * p, :, cols], preferred_element_type=F32)
            b = jnp.dot(sh1, cot[2 * p + 1, :, cols], preferred_element_type=F32)
            both = jnp.concatenate([a.reshape(16, 8, 256), b.reshape(16, 8, 256)], axis=1)
            slabs[:, p * 16 : (p + 1) * 16, cols] = both.astype(BF16)

    pl.semaphore_wait(barrier, 20)

    def s1_copy(half, g, slot):
        return pltpu.make_async_remote_copy(
            src_ref=slabs.at[half * 8 + g],
            dst_ref=landed.at[half, slot],
            send_sem=s1_send.at[half, g],
            recv_sem=s1_recv.at[half, slot],
            device_id=(ring_dev(half, g), c),
            device_id_type=MESH,
        )

    def id_copy(half, g, slot):
        return pltpu.make_async_remote_copy(
            src_ref=ids.at[half, positions[half]],
            dst_ref=ids.at[half, slot],
            send_sem=id_send.at[half, g],
            recv_sem=id_recv.at[half, slot],
            device_id=(ring_dev(half, g), c),
            device_id_type=MESH,
        )

    def s1_start(o):
        for half in range(2):
            g = lax.rem(positions[half] + o, RING)
            id_copy(half, g, positions[half]).start()
            s1_copy(half, g, positions[half]).start()

    steps(1, RING, s1_start)

    def z_copy(turn, src, dst, peer, slot):
        return pltpu.make_async_remote_copy(
            src_ref=src,
            dst_ref=dst.at[slot],
            send_sem=z_send.at[turn, peer],
            recv_sem=z_recv.at[turn, slot],
            device_id=(me, peer),
            device_id_type=MESH,
        )

    def x_copy(peer, slot):
        return z_copy(0, normed_ref, x_all, peer, slot)

    steps(1, NZ, lambda o: x_copy(lax.rem(c + o, NZ), c).start())
    x_all[c] = normed_ref[...]
    for half in range(2):
        landed[half, positions[half]] = slabs[half * 8 + positions[half]]

    loads[8].wait()
    loads[9].wait()

    def fuse(i):
        mine = rows_of(i * 128, 128)
        for n in range(4):
            cols = slice(n * 256, (n + 1) * 256)
            fused[mine, cols] = jnp.dot(
                project[mine, :], adapter[:, cols], preferred_element_type=F32
            ).astype(BF16)

    steps(0, 8, fuse)

    loads[10].wait()
    prow = lax.broadcasted_iota(jnp.int32, (256, 256), 0)
    pcol = lax.broadcasted_iota(jnp.int32, (256, 256), 1)
    want = jnp.where(prow < 128, 2 * prow, 2 * prow - 255)
    apart = (pcol == want).astype(F32).astype(BF16)
    for b in range(8):
        both = jnp.dot(apart, expand2[b * 256 : (b + 1) * 256, :], preferred_element_type=F32)
        both = both.astype(BF16)
        expand[b * 128 : (b + 1) * 128, 0:128] = both[:128]
        expand[b * 128 : (b + 1) * 128, 128:256] = both[128:]

    steps(1, NZ, lambda o: x_copy(lax.rem(c + o, NZ), lax.rem(c + o, NZ)).wait_recv())
    both = jnp.zeros((128, 256), F32)
    for b in range(8):
        both += jnp.dot(
            x_all[b], expand[b * 128 : (b + 1) * 128, :], preferred_element_type=F32
        )
    value = both[:, :128]
    sig_gate = jax.nn.sigmoid(both[:, 128:])
    frame = lax.broadcasted_iota(jnp.int32, (128, 128), 0)
    mask = (frame < frames_sm[0]).astype(F32)
    pad[...] = jnp.zeros_like(pad)
    pad[8:136, :] = mask * value * sig_gate
    taps = taps_ref[...].astype(F32)
    depth = jnp.zeros((128, 128), F32)
    for k in range(9):
        depth += taps[k : k + 1, :] * pad[4 + k : 132 + k, :]
    shifted = depth * scale_ref[...] + shift_ref[...]
    sig_shift = jax.nn.sigmoid(shifted)
    f_gsw[...] = sig_shift * (1.0 + shifted * (1.0 - sig_shift)) * scale_ref[...] * mask
    f_val[...] = sig_gate * mask
    f_gate[...] = value * sig_gate * (1.0 - sig_gate) * mask

    lane = lax.broadcasted_iota(jnp.int32, (8, 256), 1)
    same = lax.broadcasted_iota(jnp.int32, (8, 256), 0) == lax.rem(lane, 8)
    unit = lax.div(lane, 8)
    turned = (lax.rem(lax.div(unit, 2), 4) * NX + lax.div(unit, 8)) * NCORE + lax.rem(unit, 2)
    utts = (unit, turned)
    for half in range(2):

        def id_wait(o, half=half):
            slot = lax.rem(positions[half] + o, RING)
            id_copy(half, slot, slot).wait_recv()

        steps(1, RING, id_wait)

        def choose(s, half=half):
            for r in range(8):
                row = ids[half, s, r : r + 1, :]
                wide = jnp.concatenate([row, row], axis=1)
                hit = jnp.logical_and(same, wide == utts[half])
                sel_t[rows_of(s * 64 + r * 8, 8), :] = hit.astype(F32)

        steps(0, 8, choose)
        sel[half] = sel_t[...].T.astype(BF16)

    def s2_copy(half, q, slot):
        return pltpu.make_async_remote_copy(
            src_ref=part.at[half, q],
            dst_ref=part_in.at[half, slot],
            send_sem=s2_send.at[half, q],
            recv_sem=s2_recv.at[half, slot],
            device_id=(line_dev(half, q), c),
            device_id_type=MESH,
        )

    for half in range(2):

        def s1_wait(o, half=half):
            slot = lax.rem(positions[half] + o, RING)
            s1_copy(half, slot, slot).wait_recv()

        steps(1, RING, s1_wait)
        for n in range(4):
            cols = slice(n * 256, (n + 1) * 256)
            got = jnp.dot(
                sel[half],
                landed[half, :, :, cols].reshape(512, 256),
                preferred_element_type=F32,
            )
            part[half, :, :, cols] = got.astype(BF16).reshape(4, 64, 256)

        def s2_start(o, half=half):
            s2_copy(half, lax.rem(lines[half] + o, 4), lines[half]).start()

        steps(1, 4, s2_start)
        part_in[half, lines[half]] = part[half, lines[half]]

    for half in range(2):

        def s2_wait(o, half=half):
            slot = lax.rem(lines[half] + o, 4)
            s2_copy(half, slot, slot).wait_recv()

        steps(1, 4, s2_wait)
        total = part_in[half, 0].astype(F32)
        for q in range(1, 4):
            total += part_in[half, q].astype(F32)
        fg[half * 64 : (half + 1) * 64, :] = total.astype(BF16)

    for kind, weight in ((0, fused), (1, adapter)):
        for n in range(4):
            got = nt(fg[...], weight[n * 256 : (n + 1) * 256, :]).astype(BF16)
            zsend[kind, 2 * n] = got[:, :128]
            zsend[kind, 2 * n + 1] = got[:, 128:]

        def zk_start(o, kind=kind):
            peer = lax.rem(c + o, NZ)
            z_copy(1 + kind, zsend.at[kind, peer], zrecv.at[kind], peer, c).start()

        steps(1, NZ, zk_start)
        zrecv[kind, c] = zsend[kind, c]

    def back_copy(kind, half, g, slot):
        return pltpu.make_async_remote_copy(
            src_ref=owned.at[kind, rows_of(half * 64 + g * 8, 8), :],
            dst_ref=back.at[kind, rows_of(half * 64 + slot * 8, 8), :],
            send_sem=b_send.at[kind, half, g],
            recv_sem=b_recv.at[kind, half, slot],
            device_id=(ring_dev(half, g), c),
            device_id_type=MESH,
        )

    def z_sum(kind):
        def zk_wait(o):
            slot = lax.rem(c + o, NZ)
            z_copy(1 + kind, zsend.at[kind, slot], zrecv.at[kind], slot, slot).wait_recv()

        steps(1, NZ, zk_wait)
        total = zrecv[kind, 0].astype(F32)
        for b in range(1, NZ):
            total += zrecv[kind, b].astype(F32)
        return total

    def give_back(kind):
        owned[kind] = z_sum(kind)

        def go(o):
            for half in range(2):
                back_copy(kind, half, lax.rem(positions[half] + o, RING), positions[half]).start()

        steps(1, RING, go)
        for half in range(2):
            mine = rows_of(half * 64 + positions[half] * 8, 8)
            back[kind, mine, :] = owned[kind, mine, :]

    def back_wait(kind):
        def hold(o):
            for half in range(2):
                slot = lax.rem(positions[half] + o, RING)
                back_copy(kind, half, slot, slot).wait_recv()

        steps(1, RING, hold)

    give_back(0)
    back_wait(0)
    pad[8:136, :] = back[0] * f_gsw[...]
    grad_glu = jnp.zeros((128, 128), F32)
    for k in range(9):
        grad_glu += taps[k : k + 1, :] * pad[12 - k : 140 - k, :]
    grad_expanded = jnp.concatenate(
        [grad_glu * f_val[...], grad_glu * f_gate[...]], axis=1
    ).astype(BF16)
    for n in range(4):
        got = nt(grad_expanded, expand[n * 256 : (n + 1) * 256, :]).astype(BF16)
        zsend[2, 2 * n] = got[:, :128]
        zsend[2, 2 * n + 1] = got[:, 128:]

    def z2_start(o):
        peer = lax.rem(c + o, NZ)
        z_copy(3, zsend.at[2, peer], zrecv.at[2], peer, c).start()

    steps(1, NZ, z2_start)
    zrecv[2, c] = zsend[2, c]

    give_back(1)
    back_wait(1)
    stream_out[...] = (back[1] * mask).astype(BF16)
    normed_out[...] = z_sum(2).astype(BF16)

    def sent(o):
        peer = lax.rem(c + o, NZ)
        x_copy(peer, c).wait_send()
        for kind in range(3):
            z_copy(1 + kind, zsend.at[kind, peer], zrecv.at[kind], peer, c).wait_send()
        for half in range(2):
            g = lax.rem(positions[half] + o, RING)
            s1_copy(half, g, positions[half]).wait_send()
            id_copy(half, g, positions[half]).wait_send()
            for kind in range(2):
                back_copy(kind, half, g, positions[half]).wait_send()

    steps(1, NZ, sent)

    def sent_line(o):
        for half in range(2):
            s2_copy(half, lax.rem(lines[half] + o, 4), lines[half]).wait_send()

    steps(1, 4, sent_line)


def body(
    frame_cotangent,
    rollout_utterance,
    frame_offset,
    utterance_frames,
    normed_input,
    expand_weight,
    depth_kernel,
    norm_scale,
    norm_shift,
    project_weight,
    adapter_weight,
):
    smem = pl.BlockSpec(memory_space=pltpu.SMEM)
    vmem = pl.BlockSpec(memory_space=pltpu.VMEM)
    hbm = pl.BlockSpec(memory_space=pl.ANY)
    dma = pltpu.SemaphoreType.DMA
    block = jax.ShapeDtypeStruct((128, 128), BF16)
    stream, normed = pl.pallas_call(
        kernel,
        out_shape=(block, block),
        in_specs=[smem] * 3 + [vmem] * 4 + [hbm] * 4,
        out_specs=(vmem, vmem),
        scratch_shapes=[
            pltpu.VMEM((8, 160, 1024), BF16),
            pltpu.VMEM((2048, 128), BF16),
            pltpu.VMEM((1024, 1024), BF16),
            pltpu.VMEM((1024, 1024), BF16),
            pltpu.VMEM((1024, 1024), BF16),
            pltpu.VMEM((1024, 256), BF16),
            pltpu.VMEM((16, 64, 1024), BF16),
            pltpu.VMEM((2, 8, 64, 1024), BF16),
            pltpu.VMEM((2, 8, 8, 128), jnp.int32),
            pltpu.VMEM((512, 256), F32),
            pltpu.VMEM((2, 256, 512), BF16),
            pltpu.VMEM((2, 4, 64, 1024), BF16),
            pltpu.VMEM((2, 4, 64, 1024), BF16),
            pltpu.VMEM((128, 1024), BF16),
            pltpu.VMEM((8, 128, 128), BF16),
            pltpu.VMEM((3, 8, 128, 128), BF16),
            pltpu.VMEM((3, 8, 128, 128), BF16),
            pltpu.VMEM((2, 128, 128), F32),
            pltpu.VMEM((2, 128, 128), F32),
            pltpu.VMEM((144, 128), F32),
            pltpu.VMEM((128, 128), F32),
            pltpu.VMEM((128, 128), F32),
            pltpu.VMEM((128, 128), F32),
            dma((11,)),
            dma((2, 8)),
            dma((2, 8)),
            dma((2, 8)),
            dma((2, 8)),
            dma((2, 4)),
            dma((2, 4)),
            dma((4, 8)),
            dma((4, 8)),
            dma((2, 2, 8)),
            dma((2, 2, 8)),
        ],
        compiler_params=pltpu.CompilerParams(
            collective_id=0, has_side_effects=True, vmem_limit_bytes=40 * 1024 * 1024
        ),
        cost_estimate=pl.CostEstimate(
            flops=5_000_000_000, bytes_accessed=8_000_000, transcendentals=40_000
        ),
    )(
        rollout_utterance,
        frame_offset,
        utterance_frames,
        normed_input.reshape(128, 128),
        depth_kernel,
        norm_scale.reshape(1, 128),
        norm_shift.reshape(1, 128),
        frame_cotangent,
        expand_weight.reshape(2048, 128),
        project_weight,
        adapter_weight,
    )
    return stream.reshape(1, 128, 128), normed.reshape(1, 128, 128)


def solution(mesh):
    return jax.shard_map(
        body,
        mesh=mesh,
        in_specs=(
            P("dec", None, "ch"),
            P("dec"),
            P("dec"),
            P("dec"),
            P("dec", None, "ch"),
            P(None, None, "ch"),
            P(None, "ch"),
            P("ch"),
            P("ch"),
            P(),
            P(None, "ch"),
        ),
        out_specs=(P("dec", None, "ch"), P("dec", None, "ch")),
        check_vma=False,
    )
```

time: 292 us -> 71.1 us (0.24); the launches traced: 287 us -> 70.7 us
  waiting for transfers between devices: 184 us -> 0 us
  Pallas kernels: 0 us -> 58.2 us
  blocking collectives: 37.9 us -> 0 us
  local copies, waits for them, and re-layouts: 37.2 us -> 11.2 us
  between operations: 14.6 us -> 1.31 us
  matrix products: 8.12 us -> 0 us
  other arithmetic: 4.86 us -> 0 us
    unnamed x6 -> x0, waiting for transfers between devices: 184 us -> none
    pallas_call x0 -> x1, Pallas kernels: none -> 58.2 us  [body(): pl.pallas_call(kernel, out_shape=(block, block), in_specs=[smem] * 3 + [v...]
    all_gather x2 -> x0, blocking collectives: 37.9 us -> none  [the longest x1 20.5 us: body(): piece = lax.all_gather(normed_input, 'ch', axis=2, tiled=True)]
    gather x24 -> x0, local copies, waits for them, and re-layouts: 29.7 us -> none
    dot_general x5 -> x0, matrix products: 8.12 us -> none  [the longest x1 5.54 us: body(): jnp.dot(select, flat_slabs, preferred_element_type=jnp.float32)]
    reshape x2 -> x0, other arithmetic: 3.91 us -> none  [the longest x1 3.82 us: body(): received.reshape(u_local, frames, d_local) * mask[:, :, None]]
    unnamed x25 -> x22, local copies, waits for them, and re-layouts: 7.43 us -> 11.2 us
  transfers between devices with their start and end apart: 3 -> 0, of which waited for: 3 -> 0; matrix products, arithmetic and copies ran while one was open for 0% -> 0% of each run, Pallas kernels for 0% -> 0%
where the time goes in v1:
time: 71.1 us; the launch traced here: 70.7 us
  Pallas kernels  58.2 us (82%)
  local copies, waits for them, and re-layouts  11.2 us (16%)
  between operations  1.31 us (2%)
    pallas_call x1, Pallas kernels, body(): pl.pallas_call(kernel, out_shape=(block, block), in_specs=[smem] * 3 + [v...  58.2 us
    unnamed x22, local copies, waits for them, and re-layouts  11.2 us

profile of v1, /device:TPU:1, one launch (start us, length us, event | category | flops | bytes accessed | tf_op | source)
XLA Modules:
  0.0 70.7 jit_solution(6027990321152079504)
XLA Ops:
  1.3 0.0 copy-start
  1.3 1.7 %copy-done = bf16[8,160,1024]{2,1,0:T(8,128)(2,1)S(1)} copy-done((bf16[8,160,1024]{2,1,0:T(8,128)(2,1)S(1)}, bf16[8,160,1024]{2,1,0:T(8,128)(2,1)}, u32[]{:S(2)}) %copy-start) | copy-done | bytes 2621464
  3.0 0.0 copy-start.1
  3.0 1.6 %copy-done.1 = bf16[1024,1024]{1,0:T(8,128)(2,1)S(1)} copy-done((bf16[1024,1024]{1,0:T(8,128)(2,1)S(1)}, bf16[1024,1024]{1,0:T(8,128)(2,1)}, u32[]{:S(2)}) %copy-start.1) | copy-done | bytes 2097176
  4.6 0.0 copy-start.2
  4.6 1.6 %copy-done.2 = bf16[1024,1024]{1,0:T(8,128)(2,1)S(1)} copy-done((bf16[1024,1024]{1,0:T(8,128)(2,1)S(1)}, bf16[1024,1024]{1,0:T(8,128)(2,1)}, u32[]{:S(2)}) %copy-start.2) | copy-done | bytes 2097176
  6.2 0.0 copy-start.3
  6.2 1.0 %copy-done.3 = bf16[1024,2,128]{2,1,0:T(2,128)(2,1)S(1)} copy-done((bf16[1024,2,128]{2,1,0:T(2,128)(2,1)S(1)}, bf16[1024,2,128]{2,1,0:T(2,128)(2,1)}, u32[]{:S(2)}) %copy-start.3) | copy-done | bytes 524312
  7.2 0.0 copy-start.4
  7.2 0.8 %copy-done.4 = bf16[1,128,128]{2,1,0:T(8,128)(2,1)S(1)} copy-done((bf16[1,128,128]{2,1,0:T(8,128)(2,1)S(1)}, bf16[1,128,128]{2,1,0:T(8,128)(2,1)}, u32[]{:S(2)}) %copy-start.4) | copy-done | bytes 32792
  8.0 0.0 copy-start.5
  8.0 0.7 copy-done.5
  8.7 0.0 copy-start.6
  8.7 0.7 copy-done.6
  9.3 0.0 copy-start.7
  9.3 0.7 copy-done.7
  10.0 0.0 copy-start.8
  10.0 0.7 copy-done.8
  10.7 0.0 copy-start.9
  10.7 0.7 copy-done.9
  11.3 58.2 %shard_map.122 = (bf16[128,128]{1,0:T(8,128)(2,1)S(1)}, bf16[128,128]{1,0:T(8,128)(2,1)S(1)}) custom-call(s32[8]{0:T(128)S(1)} %copy-done.6, s32[8]{0:T(128)S(1)} %copy-done.7, s32[1]{0:T(128)S(6)} %copy.15.frames_sm, bf16[128,128]{1,0:T(8,128)(2,1)S(1)} %bitcast.9, bf16[9,128]{1,0:T(8,128)(2,1)S(1)} %copy-done.5, f32[1,128]{1,0:T(1,128)S(1)} %bitcast.10, ...), custom_call_target="tpu_custom_call" | custom-call | flops 5000000000 | bytes 8000000 | tf_op jit(solution)/shard_map/pallas_call | solution.py:422
  69.5 0.6 copy.16
  70.1 0.6 copy.17
Async XLA Ops:
  1.3 1.7 %copy-start = (bf16[8,160,1024]{2,1,0:T(8,128)(2,1)S(1)}, bf16[8,160,1024]{2,1,0:T(8,128)(2,1)}, u32[]{:S(2)}) copy-start(bf16[8,160,1024]{2,1,0:T(8,128)(2,1)} %cot_hbm.1) | copy-start | bytes 7864324
  3.0 1.6 %copy-start.1 = (bf16[1024,1024]{1,0:T(8,128)(2,1)S(1)}, bf16[1024,1024]{1,0:T(8,128)(2,1)}, u32[]{:S(2)}) copy-start(bf16[1024,1024]{1,0:T(8,128)(2,1)} %project_hbm.1) | copy-start | bytes 6291460
  4.6 1.6 %copy-start.2 = (bf16[1024,1024]{1,0:T(8,128)(2,1)S(1)}, bf16[1024,1024]{1,0:T(8,128)(2,1)}, u32[]{:S(2)}) copy-start(bf16[1024,1024]{1,0:T(8,128)(2,1)} %adapter_hbm.1) | copy-start | bytes 6291460
  6.2 1.0 %copy-start.3 = (bf16[1024,2,128]{2,1,0:T(2,128)(2,1)S(1)}, bf16[1024,2,128]{2,1,0:T(2,128)(2,1)}, u32[]{:S(2)}) copy-start(bf16[1024,2,128]{2,1,0:T(2,128)(2,1)} %param.16) | copy-start | bytes 1572868
  7.2 0.8 %copy-start.4 = (bf16[1,128,128]{2,1,0:T(8,128)(2,1)S(1)}, bf16[1,128,128]{2,1,0:T(8,128)(2,1)}, u32[]{:S(2)}) copy-start(bf16[1,128,128]{2,1,0:T(8,128)(2,1)} %param.15) | copy-start | bytes 98308
  8.0 0.7 copy-start.5
  8.7 0.7 copy-start.6
  9.3 0.7 copy-start.7
  10.0 0.7 copy-start.8
  10.7 0.7 copy-start.9

commit v2 on v1

--- a/solution.py
+++ b/solution.py
@@ -29,6 +29,19 @@
 
 
 def kernel(
+    ids_hbm,
+    offs_hbm,
+    frames_hbm,
+    normed_hbm,
+    taps_hbm,
+    scale_hbm,
+    shift_hbm,
+    cot_hbm,
+    expand_hbm,
+    project_hbm,
+    adapter_hbm,
+    stream_out,
+    normed_out,
     ids_sm,
     offs_sm,
     frames_sm,
@@ -36,12 +49,6 @@
     taps_ref,
     scale_ref,
     shift_ref,
-    cot_hbm,
-    expand_hbm,
-    project_hbm,
-    adapter_hbm,
-    stream_out,
-    normed_out,
     cot,
     expand2,
     project,
@@ -86,6 +93,9 @@
     pos_b = y * NCORE + core
     positions = (pos_a, pos_b)
 
+    def group(half, g):
+        return lax.rem(g, NCORE) * 8 + half * 4 + lax.div(g, NCORE)
+
     def ring_dev(half, g):
         if half == 0:
             return y * RING + g
@@ -98,14 +108,21 @@
 
     lines = (y, x)
 
-    loads = []
-    for r in range(8):
-        loads.append(pltpu.make_async_copy(cot_hbm.at[r], cot.at[r], load_sem.at[r]))
-    loads.append(pltpu.make_async_copy(project_hbm, project, load_sem.at[8]))
-    loads.append(pltpu.make_async_copy(adapter_hbm, adapter, load_sem.at[9]))
-    loads.append(pltpu.make_async_copy(expand_hbm, expand2, load_sem.at[10]))
-    for load in loads:
-        load.start()
+    small = (
+        (offs_hbm, offs_sm),
+        (ids_hbm, ids_sm),
+        (normed_hbm, normed_ref),
+        (frames_hbm, frames_sm),
+        (taps_hbm, taps_ref),
+        (scale_hbm, scale_ref),
+        (shift_hbm, shift_ref),
+    )
+    pairs = [(cot_hbm.at[r], cot.at[r]) for r in range(8)]
+    pairs += [(project_hbm, project), (adapter_hbm, adapter), (expand_hbm, expand2)]
+    pairs += small
+    loads = [pltpu.make_async_copy(a, b, load_sem.at[n]) for n, (a, b) in enumerate(pairs)]
+    for n in (11, 12, 0, 1, 2, 3, 4, 5, 6, 7, 13, 8, 9, 10, 14, 15, 16, 17):
+        loads[n].start()
 
     barrier = pltpu.get_barrier_semaphore()
 
@@ -117,6 +134,8 @@
         steps(1, NY, lambda o: greet((ring_dev(1, lax.rem(y + o, NY) * NCORE + other), c)))
     steps(1, NZ, lambda o: greet((me, lax.rem(c + o, NZ))))
 
+    loads[11].wait()
+    loads[12].wait()
     row8 = lax.broadcasted_iota(jnp.int32, (8, 128), 0)
     tile = jnp.zeros((8, 128), jnp.int32)
     for r in range(8):
@@ -143,7 +162,7 @@
 
     def s1_copy(half, g, slot):
         return pltpu.make_async_remote_copy(
-            src_ref=slabs.at[half * 8 + g],
+            src_ref=slabs.at[group(half, g)],
             dst_ref=landed.at[half, slot],
             send_sem=s1_send.at[half, g],
             recv_sem=s1_recv.at[half, slot],
@@ -161,13 +180,26 @@
             device_id_type=MESH,
         )
 
-    def s1_start(o):
+    def id_start(o):
         for half in range(2):
             g = lax.rem(positions[half] + o, RING)
             id_copy(half, g, positions[half]).start()
-            s1_copy(half, g, positions[half]).start()
-
-    steps(1, RING, s1_start)
+
+    steps(1, RING, id_start)
+    for other in range(NCORE):
+
+        def s1_start(o, other=other):
+            for half in range(2):
+                g = lax.rem(lines[1 - half] + o, 4) * NCORE + other
+                s1_copy(half, g, positions[half]).start()
+
+        steps(1, 4, s1_start)
+
+        @pl.when(core != other)
+        def _():
+            for half in range(2):
+                s1_copy(half, lines[1 - half] * NCORE + other, positions[half]).start()
+
 
     def z_copy(turn, src, dst, peer, slot):
         return pltpu.make_async_remote_copy(
@@ -182,10 +214,11 @@
     def x_copy(peer, slot):
         return z_copy(0, normed_ref, x_all, peer, slot)
 
+    loads[13].wait()
     steps(1, NZ, lambda o: x_copy(lax.rem(c + o, NZ), c).start())
     x_all[c] = normed_ref[...]
     for half in range(2):
-        landed[half, positions[half]] = slabs[half * 8 + positions[half]]
+        landed[half, positions[half]] = slabs[group(half, positions[half])]
 
     loads[8].wait()
     loads[9].wait()
@@ -201,6 +234,8 @@
     steps(0, 8, fuse)
 
     loads[10].wait()
+    for n in range(14, 18):
+        loads[n].wait()
     prow = lax.broadcasted_iota(jnp.int32, (256, 256), 0)
     pcol = lax.broadcasted_iota(jnp.int32, (256, 256), 1)
     want = jnp.where(prow < 128, 2 * prow, 2 * prow - 255)
@@ -316,7 +351,7 @@
     def back_copy(kind, half, g, slot):
         return pltpu.make_async_remote_copy(
             src_ref=owned.at[kind, rows_of(half * 64 + g * 8, 8), :],
-            dst_ref=back.at[kind, rows_of(half * 64 + slot * 8, 8), :],
+            dst_ref=back.at[kind, rows_of(group(half, slot) * 8, 8), :],
             send_sem=b_send.at[kind, half, g],
             recv_sem=b_recv.at[kind, half, slot],
             device_id=(ring_dev(half, g), c),
@@ -344,7 +379,8 @@
         steps(1, RING, go)
         for half in range(2):
             mine = rows_of(half * 64 + positions[half] * 8, 8)
-            back[kind, mine, :] = owned[kind, mine, :]
+            home = rows_of(group(half, positions[half]) * 8, 8)
+            back[kind, home, :] = owned[kind, mine, :]
 
     def back_wait(kind):
         def hold(o):
@@ -414,7 +450,6 @@
     project_weight,
     adapter_weight,
 ):
-    smem = pl.BlockSpec(memory_space=pltpu.SMEM)
     vmem = pl.BlockSpec(memory_space=pltpu.VMEM)
     hbm = pl.BlockSpec(memory_space=pl.ANY)
     dma = pltpu.SemaphoreType.DMA
@@ -422,9 +457,16 @@
     stream, normed = pl.pallas_call(
         kernel,
         out_shape=(block, block),
-        in_specs=[smem] * 3 + [vmem] * 4 + [hbm] * 4,
+        in_specs=[hbm] * 11,
         out_specs=(vmem, vmem),
         scratch_shapes=[
+            pltpu.SMEM((8,), jnp.int32),
+            pltpu.SMEM((8,), jnp.int32),
+            pltpu.SMEM((1,), jnp.int32),
+            pltpu.VMEM((128, 128), BF16),
+            pltpu.VMEM((9, 128), BF16),
+            pltpu.VMEM((1, 128), F32),
+            pltpu.VMEM((1, 128), F32),
             pltpu.VMEM((8, 160, 1024), BF16),
             pltpu.VMEM((2048, 128), BF16),
             pltpu.VMEM((1024, 1024), BF16),
@@ -448,7 +490,7 @@
             pltpu.VMEM((128, 128), F32),
             pltpu.VMEM((128, 128), F32),
             pltpu.VMEM((128, 128), F32),
-            dma((11,)),
+            dma((18,)),
             dma((2, 8)),
             dma((2, 8)),
             dma((2, 8)),
@@ -461,7 +503,7 @@
             dma((2, 2, 8)),
         ],
         compiler_params=pltpu.CompilerParams(
-            collective_id=0, has_side_effects=True, vmem_limit_bytes=40 * 1024 * 1024
+            collective_id=0, has_side_effects=True, vmem_limit_bytes=63 * 1024 * 1024
         ),
         cost_estimate=pl.CostEstimate(
             flops=5_000_000_000, bytes_accessed=8_000_000, transcendentals=40_000

time: 71.1 us -> 59 us (0.83)
  local copies, waits for them, and re-layouts: 11.2 us -> 2.75 us
  Pallas kernels: 58.2 us -> 54.7 us
    unnamed x22 -> x2, local copies, waits for them, and re-layouts: 11.2 us -> 2.75 us
    pallas_call x1, Pallas kernels: 58.2 us -> 54.7 us  [body(): pl.pallas_call(kernel, out_shape=(block, block), in_specs=[hbm] * 11, out...]
where the time goes in v2:
time: 59 us; the launch traced here: 58.8 us
  Pallas kernels  54.7 us (93%)
  local copies, waits for them, and re-layouts  2.75 us (5%)
  between operations  1.29 us (2%)
    pallas_call x1, Pallas kernels, body(): pl.pallas_call(kernel, out_shape=(block, block), in_specs=[hbm] * 11, out...  54.7 us
    unnamed x2, local copies, waits for them, and re-layouts  2.75 us

profile of v2, /device:TPU:1, one launch (start us, length us, event | category | flops | bytes accessed | tf_op | source)
XLA Modules:
  0.0 58.8 jit_solution(1656063208421626867)
XLA Ops:
  1.3 54.7 %shard_map.122 = (bf16[128,128]{1,0:T(8,128)(2,1)}, bf16[128,128]{1,0:T(8,128)(2,1)}) custom-call(s32[8]{0:T(128)} %ids_hbm.1, s32[8]{0:T(128)} %offs_hbm.1, s32[1]{0:T(128)S(6)} %copy.15.frames_hbm, bf16[128,128]{1,0:T(8,128)(2,1)} %bitcast.9, bf16[9,128]{1,0:T(8,128)(2,1)} %taps_hbm.1, f32[1,128]{1,0:T(1,128)} %bitcast.10, f32[1,128]{1,0:T(1,128)} %bitcast.11, ...), custom_call_target="tpu_custom_call" | custom-call | flops 5000000000 | bytes 8000000 | tf_op jit(solution)/shard_map/pallas_call | solution.py:457
  56.0 1.4 %copy.16 = bf16[1,128,128]{2,1,0:T(8,128)(2,1)} copy(bf16[1,128,128]{2,1,0:T(8,128)(2,1)} %bitcast.7) | data formatting | bytes 65536
  57.4 1.4 %copy.17 = bf16[1,128,128]{2,1,0:T(8,128)(2,1)} copy(bf16[1,128,128]{2,1,0:T(8,128)(2,1)} %bitcast.6) | data formatting | bytes 65536

commit v3 on v2

--- a/solution.py
+++ b/solution.py
@@ -66,6 +66,10 @@
     x_all,
     zsend,
     zrecv,
+    wsend,
+    wrecv,
+    fsend,
+    frecv,
     owned,
     back,
     pad,
@@ -271,8 +275,10 @@
     lane = lax.broadcasted_iota(jnp.int32, (8, 256), 1)
     same = lax.broadcasted_iota(jnp.int32, (8, 256), 0) == lax.rem(lane, 8)
     unit = lax.div(lane, 8)
-    turned = (lax.rem(lax.div(unit, 2), 4) * NX + lax.div(unit, 8)) * NCORE + lax.rem(unit, 2)
-    utts = (unit, turned)
+    outer = lax.div(unit, 8)
+    inner = lax.rem(unit, 4)
+    odd = lax.rem(lax.div(unit, 4), NCORE)
+    utts = ((outer * NX + inner) * NCORE + odd, (inner * NX + outer) * NCORE + odd)
     for half in range(2):
 
         def id_wait(o, half=half):
@@ -291,12 +297,12 @@
         steps(0, 8, choose)
         sel[half] = sel_t[...].T.astype(BF16)
 
-    def s2_copy(half, q, slot):
+    def s2_copy(half, to, q, slot):
         return pltpu.make_async_remote_copy(
-            src_ref=part.at[half, q],
-            dst_ref=part_in.at[half, slot],
-            send_sem=s2_send.at[half, q],
-            recv_sem=s2_recv.at[half, slot],
+            src_ref=part.at[half, q, to],
+            dst_ref=part_in.at[half, to, slot],
+            send_sem=s2_send.at[half, to, q],
+            recv_sem=s2_recv.at[half, to, slot],
             device_id=(line_dev(half, q), c),
             device_id_type=MESH,
         )
@@ -315,126 +321,206 @@
                 landed[half, :, :, cols].reshape(512, 256),
                 preferred_element_type=F32,
             )
-            part[half, :, :, cols] = got.astype(BF16).reshape(4, 64, 256)
+            part[half, :, :, :, cols] = got.astype(BF16).reshape(4, 2, 32, 256)
 
         def s2_start(o, half=half):
-            s2_copy(half, lax.rem(lines[half] + o, 4), lines[half]).start()
+            s2_copy(half, 0, lax.rem(lines[half] + o, 4), lines[half]).start()
 
         steps(1, 4, s2_start)
-        part_in[half, lines[half]] = part[half, lines[half]]
-
-    for half in range(2):
-
-        def s2_wait(o, half=half):
-            slot = lax.rem(lines[half] + o, 4)
-            s2_copy(half, slot, slot).wait_recv()
-
-        steps(1, 4, s2_wait)
-        total = part_in[half, 0].astype(F32)
-        for q in range(1, 4):
-            total += part_in[half, q].astype(F32)
-        fg[half * 64 : (half + 1) * 64, :] = total.astype(BF16)
-
-    for kind, weight in ((0, fused), (1, adapter)):
+        for to in range(2):
+            part_in[half, to, lines[half]] = part[half, lines[half], to]
+
+    def s2_start(o):
+        for half in range(2):
+            s2_copy(half, 1, lax.rem(lines[half] + o, 4), lines[half]).start()
+
+    steps(1, 4, s2_start)
+
+    def z_part(to, peer, slot):
+        return z_copy(1 + to, zsend.at[to, peer], zrecv.at[to], peer, slot)
+
+    def z_stream(peer, slot):
+        return z_copy(3, wsend.at[peer], wrecv, peer, slot)
+
+    for to in range(2):
+        for half in range(2):
+
+            def s2_wait(o, half=half, to=to):
+                slot = lax.rem(lines[half] + o, 4)
+                s2_copy(half, to, slot, slot).wait_recv()
+
+            steps(1, 4, s2_wait)
+            total = part_in[half, to, 0].astype(F32)
+            for q in range(1, 4):
+                total += part_in[half, to, q].astype(F32)
+            fg[to * 64 + half * 32 : to * 64 + half * 32 + 32, :] = total.astype(BF16)
         for n in range(4):
-            got = nt(fg[...], weight[n * 256 : (n + 1) * 256, :]).astype(BF16)
-            zsend[kind, 2 * n] = got[:, :128]
-            zsend[kind, 2 * n + 1] = got[:, 128:]
-
-        def zk_start(o, kind=kind):
-            peer = lax.rem(c + o, NZ)
-            z_copy(1 + kind, zsend.at[kind, peer], zrecv.at[kind], peer, c).start()
-
-        steps(1, NZ, zk_start)
-        zrecv[kind, c] = zsend[kind, c]
-
-    def back_copy(kind, half, g, slot):
+            got = nt(fg[to * 64 : to * 64 + 64, :], fused[n * 256 : (n + 1) * 256, :])
+            got = got.astype(BF16)
+            zsend[to, 2 * n] = got[:, :128]
+            zsend[to, 2 * n + 1] = got[:, 128:]
+
+        def part_start(o, to=to):
+            z_part(to, lax.rem(c + o, NZ), c).start()
+
+        steps(1, NZ, part_start)
+        zrecv[to, c] = zsend[to, c]
+
+    for n in range(4):
+        got = nt(fg[...], adapter[n * 256 : (n + 1) * 256, :]).astype(BF16)
+        wsend[2 * n] = got[:, :128]
+        wsend[2 * n + 1] = got[:, 128:]
+    steps(1, NZ, lambda o: z_stream(lax.rem(c + o, NZ), c).start())
+    wrecv[c] = wsend[c]
+
+    def z_sum(copy, into):
+        def hold(o):
+            slot = lax.rem(c + o, NZ)
+            copy(slot, slot).wait_recv()
+
+        steps(1, NZ, hold)
+        total = into[0].astype(F32)
+        for b in range(1, NZ):
+            total += into[b].astype(F32)
+        return total
+
+    def back_copy(kind, half, to, q, slot):
+        if half == 0:
+            device = y * RING + q * NCORE + to
+        else:
+            device = q * RING + x * NCORE + to
         return pltpu.make_async_remote_copy(
-            src_ref=owned.at[kind, rows_of(half * 64 + g * 8, 8), :],
+            src_ref=owned.at[kind, rows_of(to * 64 + half * 32 + q * 8, 8), :],
             dst_ref=back.at[kind, rows_of(group(half, slot) * 8, 8), :],
-            send_sem=b_send.at[kind, half, g],
+            send_sem=b_send.at[kind, half, to * 4 + q],
             recv_sem=b_recv.at[kind, half, slot],
-            device_id=(ring_dev(half, g), c),
+            device_id=(device, c),
             device_id_type=MESH,
         )
 
-    def z_sum(kind):
-        def zk_wait(o):
-            slot = lax.rem(c + o, NZ)
-            z_copy(1 + kind, zsend.at[kind, slot], zrecv.at[kind], slot, slot).wait_recv()
-
-        steps(1, NZ, zk_wait)
-        total = zrecv[kind, 0].astype(F32)
-        for b in range(1, NZ):
-            total += zrecv[kind, b].astype(F32)
-        return total
-
-    def give_back(kind):
-        owned[kind] = z_sum(kind)
-
+    def give_back(kind, to):
         def go(o):
             for half in range(2):
-                back_copy(kind, half, lax.rem(positions[half] + o, RING), positions[half]).start()
-
-        steps(1, RING, go)
-        for half in range(2):
-            mine = rows_of(half * 64 + positions[half] * 8, 8)
-            home = rows_of(group(half, positions[half]) * 8, 8)
-            back[kind, home, :] = owned[kind, mine, :]
-
-    def back_wait(kind):
+                q = lax.rem(lines[1 - half] + o, 4)
+                back_copy(kind, half, to, q, positions[half]).start()
+
+        steps(1, 4, go)
+
+        @pl.when(core != to)
+        def _():
+            for half in range(2):
+                back_copy(kind, half, to, lines[1 - half], positions[half]).start()
+
+        @pl.when(core == to)
+        def _():
+            for half in range(2):
+                mine = rows_of(to * 64 + half * 32 + lines[1 - half] * 8, 8)
+                home = rows_of(group(half, positions[half]) * 8, 8)
+                back[kind, home, :] = owned[kind, mine, :]
+
+    def back_wait(kind, other):
         def hold(o):
             for half in range(2):
-                slot = lax.rem(positions[half] + o, RING)
-                back_copy(kind, half, slot, slot).wait_recv()
-
-        steps(1, RING, hold)
-
-    give_back(0)
-    back_wait(0)
-    pad[8:136, :] = back[0] * f_gsw[...]
-    grad_glu = jnp.zeros((128, 128), F32)
-    for k in range(9):
-        grad_glu += taps[k : k + 1, :] * pad[12 - k : 140 - k, :]
-    grad_expanded = jnp.concatenate(
-        [grad_glu * f_val[...], grad_glu * f_gate[...]], axis=1
-    ).astype(BF16)
-    for n in range(4):
-        got = nt(grad_expanded, expand[n * 256 : (n + 1) * 256, :]).astype(BF16)
-        zsend[2, 2 * n] = got[:, :128]
-        zsend[2, 2 * n + 1] = got[:, 128:]
-
-    def z2_start(o):
-        peer = lax.rem(c + o, NZ)
-        z_copy(3, zsend.at[2, peer], zrecv.at[2], peer, c).start()
-
-    steps(1, NZ, z2_start)
-    zrecv[2, c] = zsend[2, c]
-
-    give_back(1)
-    back_wait(1)
-    stream_out[...] = (back[1] * mask).astype(BF16)
-    normed_out[...] = z_sum(2).astype(BF16)
+                slot = lax.rem(lines[1 - half] + o, 4) * NCORE + other
+                back_copy(kind, half, 0, 0, slot).wait_recv()
+
+        steps(1, 4, hold)
+
+        @pl.when(core != other)
+        def _():
+            for half in range(2):
+                back_copy(kind, half, 0, 0, lines[1 - half] * NCORE + other).wait_recv()
+
+    def last_copy(turn, peer, slot):
+        rows = slice(0, 48) if turn == 0 else slice(48, 128)
+        return pltpu.make_async_remote_copy(
+            src_ref=fsend.at[peer, rows, :],
+            dst_ref=frecv.at[slot, rows, :],
+            send_sem=z_send.at[4 + turn, peer],
+            recv_sem=z_recv.at[4 + turn, slot],
+            device_id=(me, peer),
+            device_id_type=MESH,
+        )
+
+    def last_part(turn):
+        lo, hi = (0, 48) if turn == 0 else (48, 128)
+        new = slice(turn * 64, turn * 64 + 64)
+        pad[8 + turn * 64 : 72 + turn * 64, :] = back[0, new, :] * f_gsw[new, :]
+        grad_glu = jnp.zeros((hi - lo, 128), F32)
+        for k in range(9):
+            grad_glu += taps[k : k + 1, :] * pad[12 - k + lo : 12 - k + hi, :]
+        grad_expanded = jnp.concatenate(
+            [grad_glu * f_val[lo:hi, :], grad_glu * f_gate[lo:hi, :]], axis=1
+        ).astype(BF16)
+        for n in range(4):
+            got = nt(grad_expanded, expand[n * 256 : (n + 1) * 256, :]).astype(BF16)
+            fsend[2 * n, lo:hi, :] = got[:, :128]
+            fsend[2 * n + 1, lo:hi, :] = got[:, 128:]
+        steps(1, NZ, lambda o: last_copy(turn, lax.rem(c + o, NZ), c).start())
+
+    def early():
+        back_wait(0, 0)
+        last_part(0)
+
+    pl.when(core == 1)(early)
+    for to in range(2):
+        owned[0, to * 64 : to * 64 + 64, :] = z_sum(
+            lambda peer, slot, to=to: z_part(to, peer, slot), zrecv.at[to]
+        )
+        give_back(0, to)
+    pl.when(core == 0)(early)
+    back_wait(0, 1)
+    last_part(1)
+    frecv[c] = fsend[c]
+
+    owned[1] = z_sum(z_stream, wrecv)
+    for to in range(2):
+        give_back(1, to)
+    for other in range(2):
+        back_wait(1, other)
+    stream_out[...] = back[1] * mask
+
+    def last_wait(o):
+        slot = lax.rem(c + o, NZ)
+        for turn in range(2):
+            last_copy(turn, slot, slot).wait_recv()
+
+    steps(1, NZ, last_wait)
+    total = frecv[0].astype(F32)
+    for b in range(1, NZ):
+        total += frecv[b].astype(F32)
+    normed_out[...] = total
 
     def sent(o):
         peer = lax.rem(c + o, NZ)
         x_copy(peer, c).wait_send()
-        for kind in range(3):
-            z_copy(1 + kind, zsend.at[kind, peer], zrecv.at[kind], peer, c).wait_send()
+        z_stream(peer, c).wait_send()
+        for turn in range(2):
+            z_part(turn, peer, c).wait_send()
+            last_copy(turn, peer, c).wait_send()
         for half in range(2):
             g = lax.rem(positions[half] + o, RING)
             s1_copy(half, g, positions[half]).wait_send()
             id_copy(half, g, positions[half]).wait_send()
-            for kind in range(2):
-                back_copy(kind, half, g, positions[half]).wait_send()
 
     steps(1, NZ, sent)
 
     def sent_line(o):
         for half in range(2):
-            s2_copy(half, lax.rem(lines[half] + o, 4), lines[half]).wait_send()
+            for to in range(2):
+                s2_copy(half, to, lax.rem(lines[half] + o, 4), lines[half]).wait_send()
+                q = lax.rem(lines[1 - half] + o, 4)
+                for kind in range(2):
+                    back_copy(kind, half, to, q, positions[half]).wait_send()
 
     steps(1, 4, sent_line)
+    for to in range(2):
+
+        @pl.when(core != to)
+        def _():
+            for half in range(2):
+                for kind in range(2):
+                    back_copy(kind, half, to, lines[1 - half], positions[half]).wait_send()
 
 
 def body(
@@ -453,7 +539,7 @@
     vmem = pl.BlockSpec(memory_space=pltpu.VMEM)
     hbm = pl.BlockSpec(memory_space=pl.ANY)
     dma = pltpu.SemaphoreType.DMA
-    block = jax.ShapeDtypeStruct((128, 128), BF16)
+    block = jax.ShapeDtypeStruct((128, 128), F32)
     stream, normed = pl.pallas_call(
         kernel,
         out_shape=(block, block),
@@ -478,12 +564,16 @@
             pltpu.VMEM((2, 8, 8, 128), jnp.int32),
             pltpu.VMEM((512, 256), F32),
             pltpu.VMEM((2, 256, 512), BF16),
-            pltpu.VMEM((2, 4, 64, 1024), BF16),
-            pltpu.VMEM((2, 4, 64, 1024), BF16),
+            pltpu.VMEM((2, 4, 2, 32, 1024), BF16),
+            pltpu.VMEM((2, 2, 4, 32, 1024), BF16),
             pltpu.VMEM((128, 1024), BF16),
             pltpu.VMEM((8, 128, 128), BF16),
-            pltpu.VMEM((3, 8, 128, 128), BF16),
-            pltpu.VMEM((3, 8, 128, 128), BF16),
+            pltpu.VMEM((2, 8, 64, 128), BF16),
+            pltpu.VMEM((2, 8, 64, 128), BF16),
+            pltpu.VMEM((8, 128, 128), BF16),
+            pltpu.VMEM((8, 128, 128), BF16),
+            pltpu.VMEM((8, 128, 128), BF16),
+            pltpu.VMEM((8, 128, 128), BF16),
             pltpu.VMEM((2, 128, 128), F32),
             pltpu.VMEM((2, 128, 128), F32),
             pltpu.VMEM((144, 128), F32),
@@ -495,10 +585,10 @@
             dma((2, 8)),
             dma((2, 8)),
             dma((2, 8)),
-            dma((2, 4)),
-            dma((2, 4)),
-            dma((4, 8)),
-            dma((4, 8)),
+            dma((2, 2, 4)),
+            dma((2, 2, 4)),
+            dma((6, 8)),
+            dma((6, 8)),
             dma((2, 2, 8)),
             dma((2, 2, 8)),
         ],
@@ -521,7 +611,8 @@
         project_weight,
         adapter_weight,
     )
-    return stream.reshape(1, 128, 128), normed.reshape(1, 128, 128)
+    stream, normed = lax.optimization_barrier((stream, normed))
+    return stream.reshape(1, 128, 128).astype(BF16), normed.reshape(1, 128, 128).astype(BF16)
 
 
 def solution(mesh):

time: 59 us -> 56.2 us (0.953)
  local copies, waits for them, and re-layouts: 2.75 us -> 0 us
  other arithmetic: 0 us -> 1.51 us
  Pallas kernels: 54.7 us -> 53.3 us
    unnamed x2 -> x0, local copies, waits for them, and re-layouts: 2.75 us -> none
    convert_element_type x0 -> x1, other arithmetic: none -> 1.51 us  [body(): normed.reshape(1, 128, 128).astype(BF16)]
    pallas_call x1, Pallas kernels: 54.7 us -> 53.3 us  [body(): pl.pallas_call(kernel, out_shape=(block, block), in_specs=[hbm] * 11, out...]
where the time goes in v3:
time: 56.2 us; the launch traced here: 56.1 us
  Pallas kernels  53.3 us (95%)
  other arithmetic  1.51 us (3%)
  between operations  1.29 us (2%)
    pallas_call x1, Pallas kernels, body(): pl.pallas_call(kernel, out_shape=(block, block), in_specs=[hbm] * 11, out...  53.3 us
    convert_element_type x1, other arithmetic, body(): normed.reshape(1, 128, 128).astype(BF16)  1.51 us

profile of v3, /device:TPU:1, one launch (start us, length us, event | category | flops | bytes accessed | tf_op | source)
XLA Modules:
  0.0 56.1 jit_solution(13527094235807116276)
XLA Ops:
  1.3 53.3 %shard_map.122 = (f32[128,128]{1,0:T(8,128)}, f32[128,128]{1,0:T(8,128)}) custom-call(s32[8]{0:T(128)} %ids_hbm.1, s32[8]{0:T(128)} %offs_hbm.1, s32[1]{0:T(128)S(6)} %copy.13.frames_hbm, bf16[128,128]{1,0:T(8,128)(2,1)} %bitcast.9, bf16[9,128]{1,0:T(8,128)(2,1)} %taps_hbm.1, f32[1,128]{1,0:T(1,128)} %bitcast.10, f32[1,128]{1,0:T(1,128)} %bitcast.11, ...), custom_call_target="tpu_custom_call" | custom-call | flops 5000000000 | bytes 8000000 | tf_op jit(solution)/shard_map/pallas_call | solution.py:543
  54.5 1.5 %convert_bitcast_fusion = (bf16[1,128,128]{2,1,0:T(8,128)(2,1)}, bf16[1,128,128]{2,1,0:T(8,128)(2,1)}) fusion(f32[128,128]{1,0:T(8,128)} %get-tuple-element.5, f32[128,128]{1,0:T(8,128)} %get-tuple-element.4), kind=kLoop, calls=%fused_computation | loop fusion | flops 32768 | bytes 196608 | tf_op jit(solution)/shard_map/convert_element_type | solution.py:615

commit v4 on v3

--- a/solution.py
+++ b/solution.py
@@ -9,6 +9,7 @@
 F32 = jnp.float32
 BF16 = jnp.bfloat16
 NY, NX, NCORE, NZ = 4, 4, 2, 8
+FAR_FIRST = (4, 3, 5, 2, 6, 1, 7)
 RING = NX * NCORE
 
 
@@ -189,21 +190,28 @@
             g = lax.rem(positions[half] + o, RING)
             id_copy(half, g, positions[half]).start()
 
-    steps(1, RING, id_start)
-    for other in range(NCORE):
-
-        def s1_start(o, other=other):
+    def s1_out(other, offsets):
+        for o in offsets:
             for half in range(2):
                 g = lax.rem(lines[1 - half] + o, 4) * NCORE + other
                 s1_copy(half, g, positions[half]).start()
 
-        steps(1, 4, s1_start)
-
-        @pl.when(core != other)
-        def _():
-            for half in range(2):
-                s1_copy(half, lines[1 - half] * NCORE + other, positions[half]).start()
-
+    def s1_beside(other):
+        for half in range(2):
+            s1_copy(half, lines[1 - half] * NCORE + other, positions[half]).start()
+
+    steps(1, RING, id_start)
+    s1_out(0, (2, 1, 3))
+    pl.when(core == 1)(lambda: s1_beside(0))
+    s1_out(1, (1, 3))
+
+    @pl.when(core == 1)
+    def _():
+        s1_out(1, (2,))
+
+    @pl.when(core == 0)
+    def _():
+        s1_beside(1)
 
     def z_copy(turn, src, dst, peer, slot):
         return pltpu.make_async_remote_copy(
@@ -219,7 +227,8 @@
         return z_copy(0, normed_ref, x_all, peer, slot)
 
     loads[13].wait()
-    steps(1, NZ, lambda o: x_copy(lax.rem(c + o, NZ), c).start())
+    for o in FAR_FIRST:
+        x_copy(lax.rem(c + o, NZ), c).start()
     x_all[c] = normed_ref[...]
     for half in range(2):
         landed[half, positions[half]] = slabs[group(half, positions[half])]
@@ -249,6 +258,75 @@
         both = both.astype(BF16)
         expand[b * 128 : (b + 1) * 128, 0:128] = both[:128]
         expand[b * 128 : (b + 1) * 128, 128:256] = both[128:]
+
+    lane = lax.broadcasted_iota(jnp.int32, (8, 256), 1)
+    same = lax.broadcasted_iota(jnp.int32, (8, 256), 0) == lax.rem(lane, 8)
+    unit = lax.div(lane, 8)
+    outer = lax.div(unit, 8)
+    inner = lax.rem(unit, 4)
+    odd = lax.rem(lax.div(unit, 4), NCORE)
+    utts = ((outer * NX + inner) * NCORE + odd, (inner * NX + outer) * NCORE + odd)
+    for half in range(2):
+
+        def id_wait(o, half=half):
+            slot = lax.rem(positions[half] + o, RING)
+            id_copy(half, slot, slot).wait_recv()
+
+        steps(1, RING, id_wait)
+
+        def choose(s, half=half):
+            for r in range(8):
+                row = ids[half, s, r : r + 1, :]
+                wide = jnp.concatenate([row, row], axis=1)
+                hit = jnp.logical_and(same, wide == utts[half])
+                sel_t[rows_of(s * 64 + r * 8, 8), :] = hit.astype(F32)
+
+        steps(0, 8, choose)
+        sel[half] = sel_t[...].T.astype(BF16)
+
+    def s2_copy(half, to, q, slot):
+        return pltpu.make_async_remote_copy(
+            src_ref=part.at[half, q, to],
+            dst_ref=part_in.at[half, to, slot],
+            send_sem=s2_send.at[half, to, q],
+            recv_sem=s2_recv.at[half, to, slot],
+            device_id=(line_dev(half, q), c),
+            device_id_type=MESH,
+        )
+
+    for half in range(2):
+
+        def s1_wait(o, half=half):
+            slot = lax.rem(positions[half] + o, RING)
+            s1_copy(half, slot, slot).wait_recv()
+
+        steps(1, RING, s1_wait)
+        for n in range(4):
+            cols = slice(n * 256, (n + 1) * 256)
+            got = jnp.dot(
+                sel[half],
+                landed[half, :, :, cols].reshape(512, 256),
+                preferred_element_type=F32,
+            )
+            part[half, :, :, :, cols] = got.astype(BF16).reshape(4, 2, 32, 256)
+
+        def s2_start(o, half=half):
+            s2_copy(half, 0, lax.rem(lines[half] + o, 4), lines[half]).start()
+
+        steps(1, 4, s2_start)
+        for to in range(2):
+            part_in[half, to, lines[half]] = part[half, lines[half], to]
+
+    def s2_start(o):
+        for half in range(2):
+            s2_copy(half, 1, lax.rem(lines[half] + o, 4), lines[half]).start()
+
+    steps(1, 4, s2_start)
+
+    @pl.when(core == 0)
+    def _():
+        s1_out(1, (2,))
+
 
     steps(1, NZ, lambda o: x_copy(lax.rem(c + o, NZ), lax.rem(c + o, NZ)).wait_recv())
     both = jnp.zeros((128, 256), F32)
@@ -272,70 +350,6 @@
     f_val[...] = sig_gate * mask
     f_gate[...] = value * sig_gate * (1.0 - sig_gate) * mask
 
-    lane = lax.broadcasted_iota(jnp.int32, (8, 256), 1)
-    same = lax.broadcasted_iota(jnp.int32, (8, 256), 0) == lax.rem(lane, 8)
-    unit = lax.div(lane, 8)
-    outer = lax.div(unit, 8)
-    inner = lax.rem(unit, 4)
-    odd = lax.rem(lax.div(unit, 4), NCORE)
-    utts = ((outer * NX + inner) * NCORE + odd, (inner * NX + outer) * NCORE + odd)
-    for half in range(2):
-
-        def id_wait(o, half=half):
-            slot = lax.rem(positions[half] + o, RING)
-            id_copy(half, slot, slot).wait_recv()
-
-        steps(1, RING, id_wait)
-
-        def choose(s, half=half):
-            for r in range(8):
-                row = ids[half, s, r : r + 1, :]
-                wide = jnp.concatenate([row, row], axis=1)
-                hit = jnp.logical_and(same, wide == utts[half])
-                sel_t[rows_of(s * 64 + r * 8, 8), :] = hit.astype(F32)
-
-        steps(0, 8, choose)
-        sel[half] = sel_t[...].T.astype(BF16)
-
-    def s2_copy(half, to, q, slot):
-        return pltpu.make_async_remote_copy(
-            src_ref=part.at[half, q, to],
-            dst_ref=part_in.at[half, to, slot],
-            send_sem=s2_send.at[half, to, q],
-            recv_sem=s2_recv.at[half, to, slot],
-            device_id=(line_dev(half, q), c),
-            device_id_type=MESH,
-        )
-
-    for half in range(2):
-
-        def s1_wait(o, half=half):
-            slot = lax.rem(positions[half] + o, RING)
-            s1_copy(half, slot, slot).wait_recv()
-
-        steps(1, RING, s1_wait)
-        for n in range(4):
-            cols = slice(n * 256, (n + 1) * 256)
-            got = jnp.dot(
-                sel[half],
-                landed[half, :, :, cols].reshape(512, 256),
-                preferred_element_type=F32,
-            )
-            part[half, :, :, :, cols] = got.astype(BF16).reshape(4, 2, 32, 256)
-
-        def s2_start(o, half=half):
-            s2_copy(half, 0, lax.rem(lines[half] + o, 4), lines[half]).start()
-
-        steps(1, 4, s2_start)
-        for to in range(2):
-            part_in[half, to, lines[half]] = part[half, lines[half], to]
-
-    def s2_start(o):
-        for half in range(2):
-            s2_copy(half, 1, lax.rem(lines[half] + o, 4), lines[half]).start()
-
-    steps(1, 4, s2_start)
-
     def z_part(to, peer, slot):
         return z_copy(1 + to, zsend.at[to, peer], zrecv.at[to], peer, slot)
 
@@ -354,24 +368,21 @@
             for q in range(1, 4):
                 total += part_in[half, to, q].astype(F32)
             fg[to * 64 + half * 32 : to * 64 + half * 32 + 32, :] = total.astype(BF16)
-        for n in range(4):
-            got = nt(fg[to * 64 : to * 64 + 64, :], fused[n * 256 : (n + 1) * 256, :])
+
+        def send_pair(n, to=to):
+            got = nt(fg[to * 64 : to * 64 + 64, :], fused[rows_of(n * 256, 256), :])
             got = got.astype(BF16)
-            zsend[to, 2 * n] = got[:, :128]
-            zsend[to, 2 * n + 1] = got[:, 128:]
-
-        def part_start(o, to=to):
-            z_part(to, lax.rem(c + o, NZ), c).start()
-
-        steps(1, NZ, part_start)
+            for side in range(2):
+                peer = 2 * n + side
+                zsend[to, peer] = got[:, side * 128 : side * 128 + 128]
+
+                @pl.when(peer != c)
+                def _():
+                    z_part(to, peer, c).start()
+
+        for o in (2, 1, 3, 0):
+            send_pair(lax.rem(lax.div(c, 2) + o, 4))
         zrecv[to, c] = zsend[to, c]
-
-    for n in range(4):
-        got = nt(fg[...], adapter[n * 256 : (n + 1) * 256, :]).astype(BF16)
-        wsend[2 * n] = got[:, :128]
-        wsend[2 * n + 1] = got[:, 128:]
-    steps(1, NZ, lambda o: z_stream(lax.rem(c + o, NZ), c).start())
-    wrecv[c] = wsend[c]
 
     def z_sum(copy, into):
         def hold(o):
@@ -452,17 +463,31 @@
         grad_expanded = jnp.concatenate(
             [grad_glu * f_val[lo:hi, :], grad_glu * f_gate[lo:hi, :]], axis=1
         ).astype(BF16)
-        for n in range(4):
-            got = nt(grad_expanded, expand[n * 256 : (n + 1) * 256, :]).astype(BF16)
-            fsend[2 * n, lo:hi, :] = got[:, :128]
-            fsend[2 * n + 1, lo:hi, :] = got[:, 128:]
-        steps(1, NZ, lambda o: last_copy(turn, lax.rem(c + o, NZ), c).start())
+        for o in (2, 1, 3, 0):
+            n = lax.rem(lax.div(c, 2) + o, 4)
+            got = nt(grad_expanded, expand[rows_of(n * 256, 256), :]).astype(BF16)
+            for side in range(2):
+                peer = 2 * n + side
+                fsend[peer, lo:hi, :] = got[:, side * 128 : side * 128 + 128]
+
+                @pl.when(peer != c)
+                def _():
+                    last_copy(turn, peer, c).start()
 
     def early():
         back_wait(0, 0)
         last_part(0)
 
     pl.when(core == 1)(early)
+
+    for n in range(4):
+        got = nt(fg[...], adapter[n * 256 : (n + 1) * 256, :]).astype(BF16)
+        wsend[2 * n] = got[:, :128]
+        wsend[2 * n + 1] = got[:, 128:]
+    for o in FAR_FIRST:
+        z_stream(lax.rem(c + o, NZ), c).start()
+    wrecv[c] = wsend[c]
+
     for to in range(2):
         owned[0, to * 64 : to * 64 + 64, :] = z_sum(
             lambda peer, slot, to=to: z_part(to, peer, slot), zrecv.at[to]

time: 56.2 us -> 54.3 us (0.966)
  Pallas kernels: 53.3 us -> 51.3 us
    pallas_call x1, Pallas kernels: 53.3 us -> 51.3 us  [body(): pl.pallas_call(kernel, out_shape=(block, block), in_specs=[hbm] * 11, out...]
where the time goes in v4:
time: 54.3 us; the launch traced here: 54.1 us
  Pallas kernels  51.3 us (94%)
  other arithmetic  1.51 us (3%)
  between operations  1.29 us (2%)
    pallas_call x1, Pallas kernels, body(): pl.pallas_call(kernel, out_shape=(block, block), in_specs=[hbm] * 11, out...  51.3 us
    convert_element_type x1, other arithmetic, body(): normed.reshape(1, 128, 128).astype(BF16)  1.51 us

profile of v4, /device:TPU:1, one launch (start us, length us, event | category | flops | bytes accessed | tf_op | source)
XLA Modules:
  0.0 54.1 jit_solution(9486320561881624981)
XLA Ops:
  1.3 51.3 %shard_map.122 = (f32[128,128]{1,0:T(8,128)}, f32[128,128]{1,0:T(8,128)}) custom-call(s32[8]{0:T(128)} %ids_hbm.1, s32[8]{0:T(128)} %offs_hbm.1, s32[1]{0:T(128)S(6)} %copy.13.frames_hbm, bf16[128,128]{1,0:T(8,128)(2,1)} %bitcast.9, bf16[9,128]{1,0:T(8,128)(2,1)} %taps_hbm.1, f32[1,128]{1,0:T(1,128)} %bitcast.10, f32[1,128]{1,0:T(1,128)} %bitcast.11, ...), custom_call_target="tpu_custom_call" | custom-call | flops 5000000000 | bytes 8000000 | tf_op jit(solution)/shard_map/pallas_call | solution.py:568
  52.6 1.5 %convert_bitcast_fusion = (bf16[1,128,128]{2,1,0:T(8,128)(2,1)}, bf16[1,128,128]{2,1,0:T(8,128)(2,1)}) fusion(f32[128,128]{1,0:T(8,128)} %get-tuple-element.5, f32[128,128]{1,0:T(8,128)} %get-tuple-element.4), kind=kLoop, calls=%fused_computation | loop fusion | flops 32768 | bytes 196608 | tf_op jit(solution)/shard_map/convert_element_type | solution.py:640

commit v5 on v4

--- a/solution.py
+++ b/solution.py
@@ -122,11 +122,11 @@
         (scale_hbm, scale_ref),
         (shift_hbm, shift_ref),
     )
-    pairs = [(cot_hbm.at[r], cot.at[r]) for r in range(8)]
+    pairs = [(cot_hbm.at[2 * p : 2 * p + 2], cot.at[2 * p : 2 * p + 2]) for p in range(4)]
     pairs += [(project_hbm, project), (adapter_hbm, adapter), (expand_hbm, expand2)]
     pairs += small
     loads = [pltpu.make_async_copy(a, b, load_sem.at[n]) for n, (a, b) in enumerate(pairs)]
-    for n in (11, 12, 0, 1, 2, 3, 4, 5, 6, 7, 13, 8, 9, 10, 14, 15, 16, 17):
+    for n in (7, 8, 0, 1, 2, 3):
         loads[n].start()
 
     barrier = pltpu.get_barrier_semaphore()
@@ -139,8 +139,10 @@
         steps(1, NY, lambda o: greet((ring_dev(1, lax.rem(y + o, NY) * NCORE + other), c)))
     steps(1, NZ, lambda o: greet((me, lax.rem(c + o, NZ))))
 
-    loads[11].wait()
-    loads[12].wait()
+    for n in (9, 4, 5, 6, 10, 11, 12, 13):
+        loads[n].start()
+    loads[7].wait()
+    loads[8].wait()
     row8 = lax.broadcasted_iota(jnp.int32, (8, 128), 0)
     tile = jnp.zeros((8, 128), jnp.int32)
     for r in range(8):
@@ -152,8 +154,7 @@
     scol = lax.broadcasted_iota(jnp.int32, (128, 160), 1)
     diff = scol - srow
     for p in range(4):
-        loads[2 * p].wait()
-        loads[2 * p + 1].wait()
+        loads[p].wait()
         sh0 = (diff == offs_sm[2 * p]).astype(F32).astype(BF16)
         sh1 = (diff == offs_sm[2 * p + 1]).astype(F32).astype(BF16)
         for n in range(4):
@@ -200,8 +201,9 @@
         for half in range(2):
             s1_copy(half, lines[1 - half] * NCORE + other, positions[half]).start()
 
+    s1_out(0, (2,))
     steps(1, RING, id_start)
-    s1_out(0, (2, 1, 3))
+    s1_out(0, (1, 3))
     pl.when(core == 1)(lambda: s1_beside(0))
     s1_out(1, (1, 3))
 
@@ -226,15 +228,15 @@
     def x_copy(peer, slot):
         return z_copy(0, normed_ref, x_all, peer, slot)
 
-    loads[13].wait()
+    loads[9].wait()
     for o in FAR_FIRST:
         x_copy(lax.rem(c + o, NZ), c).start()
     x_all[c] = normed_ref[...]
     for half in range(2):
         landed[half, positions[half]] = slabs[group(half, positions[half])]
 
-    loads[8].wait()
-    loads[9].wait()
+    loads[4].wait()
+    loads[5].wait()
 
     def fuse(i):
         mine = rows_of(i * 128, 128)
@@ -246,8 +248,8 @@
 
     steps(0, 8, fuse)
 
-    loads[10].wait()
-    for n in range(14, 18):
+    loads[6].wait()
+    for n in range(10, 14):
         loads[n].wait()
     prow = lax.broadcasted_iota(jnp.int32, (256, 256), 0)
     pcol = lax.broadcasted_iota(jnp.int32, (256, 256), 1)
@@ -313,7 +315,8 @@
         def s2_start(o, half=half):
             s2_copy(half, 0, lax.rem(lines[half] + o, 4), lines[half]).start()
 
-        steps(1, 4, s2_start)
+        for o in (2, 1, 3):
+            s2_start(o)
         for to in range(2):
             part_in[half, to, lines[half]] = part[half, lines[half], to]
 
@@ -321,7 +324,8 @@
         for half in range(2):
             s2_copy(half, 1, lax.rem(lines[half] + o, 4), lines[half]).start()
 
-    steps(1, 4, s2_start)
+    for o in (2, 1, 3):
+        s2_start(o)
 
     @pl.when(core == 0)
     def _():
@@ -415,7 +419,8 @@
                 q = lax.rem(lines[1 - half] + o, 4)
                 back_copy(kind, half, to, q, positions[half]).start()
 
-        steps(1, 4, go)
+        for o in (2, 1, 3):
+            go(o)
 
         @pl.when(core != to)
         def _():
@@ -505,16 +510,18 @@
         back_wait(1, other)
     stream_out[...] = back[1] * mask
 
-    def last_wait(o):
-        slot = lax.rem(c + o, NZ)
-        for turn in range(2):
+    for turn in range(2):
+        lo, hi = (0, 48) if turn == 0 else (48, 128)
+
+        def last_wait(o, turn=turn):
+            slot = lax.rem(c + o, NZ)
             last_copy(turn, slot, slot).wait_recv()
 
-    steps(1, NZ, last_wait)
-    total = frecv[0].astype(F32)
-    for b in range(1, NZ):
-        total += frecv[b].astype(F32)
-    normed_out[...] = total
+        steps(1, NZ, last_wait)
+        total = frecv[0, lo:hi, :].astype(F32)
+        for b in range(1, NZ):
+            total += frecv[b, lo:hi, :].astype(F32)
+        normed_out[lo:hi, :] = total
 
     def sent(o):
         peer = lax.rem(c + o, NZ)
@@ -605,7 +612,7 @@
             pltpu.VMEM((128, 128), F32),
             pltpu.VMEM((128, 128), F32),
             pltpu.VMEM((128, 128), F32),
-            dma((18,)),
+            dma((14,)),
             dma((2, 8)),
             dma((2, 8)),
             dma((2, 8)),

time: 54.3 us -> 53.6 us (0.987)
  Pallas kernels: 51.3 us -> 50.7 us
    pallas_call x1, Pallas kernels: 51.3 us -> 50.7 us  [body(): pl.pallas_call(kernel, out_shape=(block, block), in_specs=[hbm] * 11, out...]
where the time goes in v5:
time: 53.6 us; the launch traced here: 53.5 us
  Pallas kernels  50.7 us (95%)
  other arithmetic  1.51 us (3%)
  between operations  1.29 us (2%)
    pallas_call x1, Pallas kernels, body(): pl.pallas_call(kernel, out_shape=(block, block), in_specs=[hbm] * 11, out...  50.7 us
    convert_element_type x1, other arithmetic, body(): normed.reshape(1, 128, 128).astype(BF16)  1.51 us

profile of v5, /device:TPU:1, one launch (start us, length us, event | category | flops | bytes accessed | tf_op | source)
XLA Modules:
  0.0 53.5 jit_solution(1146081512754111187)
XLA Ops:
  1.3 50.7 %shard_map.122 = (f32[128,128]{1,0:T(8,128)}, f32[128,128]{1,0:T(8,128)}) custom-call(s32[8]{0:T(128)} %ids_hbm.1, s32[8]{0:T(128)} %offs_hbm.1, s32[1]{0:T(128)S(6)} %copy.13.frames_hbm, bf16[128,128]{1,0:T(8,128)(2,1)} %bitcast.9, bf16[9,128]{1,0:T(8,128)(2,1)} %taps_hbm.1, f32[1,128]{1,0:T(1,128)} %bitcast.10, f32[1,128]{1,0:T(1,128)} %bitcast.11, ...), custom_call_target="tpu_custom_call" | custom-call | flops 5000000000 | bytes 8000000 | tf_op jit(solution)/shard_map/pallas_call | solution.py:575
  52.0 1.5 %convert_bitcast_fusion = (bf16[1,128,128]{2,1,0:T(8,128)(2,1)}, bf16[1,128,128]{2,1,0:T(8,128)(2,1)}) fusion(f32[128,128]{1,0:T(8,128)} %get-tuple-element.5, f32[128,128]{1,0:T(8,128)} %get-tuple-element.4), kind=kLoop, calls=%fused_computation | loop fusion | flops 32768 | bytes 196608 | tf_op jit(solution)/shard_map/convert_element_type | solution.py:647

commit v6 on v5

--- a/solution.py
+++ b/solution.py
@@ -264,9 +264,9 @@
     lane = lax.broadcasted_iota(jnp.int32, (8, 256), 1)
     same = lax.broadcasted_iota(jnp.int32, (8, 256), 0) == lax.rem(lane, 8)
     unit = lax.div(lane, 8)
-    outer = lax.div(unit, 8)
+    outer = lax.rem(lax.div(unit, 4), 4)
     inner = lax.rem(unit, 4)
-    odd = lax.rem(lax.div(unit, 4), NCORE)
+    odd = lax.div(unit, 16)
     utts = ((outer * NX + inner) * NCORE + odd, (inner * NX + outer) * NCORE + odd)
     for half in range(2):
 
@@ -296,36 +296,26 @@
             device_id_type=MESH,
         )
 
-    for half in range(2):
-
-        def s1_wait(o, half=half):
-            slot = lax.rem(positions[half] + o, RING)
-            s1_copy(half, slot, slot).wait_recv()
-
-        steps(1, RING, s1_wait)
-        for n in range(4):
-            cols = slice(n * 256, (n + 1) * 256)
-            got = jnp.dot(
-                sel[half],
-                landed[half, :, :, cols].reshape(512, 256),
-                preferred_element_type=F32,
-            )
-            part[half, :, :, :, cols] = got.astype(BF16).reshape(4, 2, 32, 256)
-
-        def s2_start(o, half=half):
-            s2_copy(half, 0, lax.rem(lines[half] + o, 4), lines[half]).start()
-
-        for o in (2, 1, 3):
-            s2_start(o)
-        for to in range(2):
+    for to in range(2):
+        for half in range(2):
+            if to == 0:
+
+                def s1_wait(o, half=half):
+                    slot = lax.rem(positions[half] + o, RING)
+                    s1_copy(half, slot, slot).wait_recv()
+
+                steps(1, RING, s1_wait)
+            for n in range(4):
+                cols = slice(n * 256, (n + 1) * 256)
+                got = jnp.dot(
+                    sel[half, to * 128 : to * 128 + 128, :],
+                    landed[half, :, :, cols].reshape(512, 256),
+                    preferred_element_type=F32,
+                )
+                part[half, :, to, :, cols] = got.astype(BF16).reshape(4, 32, 256)
+            for o in (2, 1, 3):
+                s2_copy(half, to, lax.rem(lines[half] + o, 4), lines[half]).start()
             part_in[half, to, lines[half]] = part[half, lines[half], to]
-
-    def s2_start(o):
-        for half in range(2):
-            s2_copy(half, 1, lax.rem(lines[half] + o, 4), lines[half]).start()
-
-    for o in (2, 1, 3):
-        s2_start(o)
 
     @pl.when(core == 0)
     def _():

time: 53.6 us -> 52.9 us (0.987)
  Pallas kernels: 50.7 us -> 50 us
    pallas_call x1, Pallas kernels: 50.7 us -> 50 us  [body(): pl.pallas_call(kernel, out_shape=(block, block), in_specs=[hbm] * 11, out...]
where the time goes in v6:
time: 52.9 us; the launch traced here: 52.8 us
  Pallas kernels  50 us (95%)
  other arithmetic  1.51 us (3%)
  between operations  1.29 us (2%)
    pallas_call x1, Pallas kernels, body(): pl.pallas_call(kernel, out_shape=(block, block), in_specs=[hbm] * 11, out...  50 us
    convert_element_type x1, other arithmetic, body(): normed.reshape(1, 128, 128).astype(BF16)  1.51 us

profile of v6, /device:TPU:1, one launch (start us, length us, event | category | flops | bytes accessed | tf_op | source)
XLA Modules:
  0.0 52.8 jit_solution(13057873133161055328)
XLA Ops:
  1.3 50.0 %shard_map.122 = (f32[128,128]{1,0:T(8,128)}, f32[128,128]{1,0:T(8,128)}) custom-call(s32[8]{0:T(128)} %ids_hbm.1, s32[8]{0:T(128)} %offs_hbm.1, s32[1]{0:T(128)S(6)} %copy.13.frames_hbm, bf16[128,128]{1,0:T(8,128)(2,1)} %bitcast.9, bf16[9,128]{1,0:T(8,128)(2,1)} %taps_hbm.1, f32[1,128]{1,0:T(1,128)} %bitcast.10, f32[1,128]{1,0:T(1,128)} %bitcast.11, ...), custom_call_target="tpu_custom_call" | custom-call | flops 5000000000 | bytes 8000000 | tf_op jit(solution)/shard_map/pallas_call | solution.py:565
  51.2 1.5 %convert_bitcast_fusion = (bf16[1,128,128]{2,1,0:T(8,128)(2,1)}, bf16[1,128,128]{2,1,0:T(8,128)(2,1)}) fusion(f32[128,128]{1,0:T(8,128)} %get-tuple-element.5, f32[128,128]{1,0:T(8,128)} %get-tuple-element.4), kind=kLoop, calls=%fused_computation | loop fusion | flops 32768 | bytes 196608 | tf_op jit(solution)/shard_map/convert_element_type | solution.py:637

commit v7 on v6

--- a/solution.py
+++ b/solution.py
@@ -473,7 +473,6 @@
         back_wait(0, 0)
         last_part(0)
 
-    pl.when(core == 1)(early)
 
     for n in range(4):
         got = nt(fg[...], adapter[n * 256 : (n + 1) * 256, :]).astype(BF16)
@@ -488,7 +487,7 @@
             lambda peer, slot, to=to: z_part(to, peer, slot), zrecv.at[to]
         )
         give_back(0, to)
-    pl.when(core == 0)(early)
+    early()
     back_wait(0, 1)
     last_part(1)
     frecv[c] = fsend[c]

time: 52.9 us -> 53.6 us (1.013)
  Pallas kernels: 50 us -> 50.7 us
    pallas_call x1, Pallas kernels: 50 us -> 50.7 us  [body(): pl.pallas_call(kernel, out_shape=(block, block), in_specs=[hbm] * 11, out...]
where the time goes in v7:
time: 53.6 us; the launch traced here: 53.5 us
  Pallas kernels  50.7 us (95%)
  other arithmetic  1.51 us (3%)
  between operations  1.29 us (2%)
    pallas_call x1, Pallas kernels, body(): pl.pallas_call(kernel, out_shape=(block, block), in_specs=[hbm] * 11, out...  50.7 us
    convert_element_type x1, other arithmetic, body(): normed.reshape(1, 128, 128).astype(BF16)  1.51 us

profile of v7, /device:TPU:1, one launch (start us, length us, event | category | flops | bytes accessed | tf_op | source)
XLA Modules:
  0.0 53.5 jit_solution(14260616523647273609)
XLA Ops:
  1.3 50.7 %shard_map.122 = (f32[128,128]{1,0:T(8,128)}, f32[128,128]{1,0:T(8,128)}) custom-call(s32[8]{0:T(128)} %ids_hbm.1, s32[8]{0:T(128)} %offs_hbm.1, s32[1]{0:T(128)S(6)} %copy.13.frames_hbm, bf16[128,128]{1,0:T(8,128)(2,1)} %bitcast.9, bf16[9,128]{1,0:T(8,128)(2,1)} %taps_hbm.1, f32[1,128]{1,0:T(1,128)} %bitcast.10, f32[1,128]{1,0:T(1,128)} %bitcast.11, ...), custom_call_target="tpu_custom_call" | custom-call | flops 5000000000 | bytes 8000000 | tf_op jit(solution)/shard_map/pallas_call | solution.py:564
  52.0 1.5 %convert_bitcast_fusion = (bf16[1,128,128]{2,1,0:T(8,128)(2,1)}, bf16[1,128,128]{2,1,0:T(8,128)(2,1)}) fusion(f32[128,128]{1,0:T(8,128)} %get-tuple-element.5, f32[128,128]{1,0:T(8,128)} %get-tuple-element.4), kind=kLoop, calls=%fused_computation | loop fusion | flops 32768 | bytes 196608 | tf_op jit(solution)/shard_map/convert_element_type | solution.py:636
